TPU v7x, 32 devices: a whole 2x2x4 slice. The times are simulated.
32 devices in a mesh: dp: 8 (over z, x), row: 4 (over y, core).
Axes of the slice: x: 2, y: 2, z: 4, core: 2. Of those that a mesh axis runs over, the one named last changes fastest.
Arguments:
- image: bfloat16 [2, 64, 28, 28, 256], P(None, 'dp', 'row'), may hold values from -6 to 6
- tags: bfloat16 [2, 64, 128, 512], P(None, ('dp', 'row')), may hold values from -6 to 6
- tag_lengths: int32 [2, 64], P(None, ('dp', 'row')), may hold values from 40 to 128, as said below
- cotangent: bfloat16 [2, 64, 128, 512], P(None, ('dp', 'row')), may hold values from -6 to 6
- conv_weight: bfloat16 [2, 3, 3, 256, 256], replicated, may hold values from -0.125 to 0.125
- bn_mean: float32 [2, 256], replicated, may hold values from -3 to 3
- bn_var: float32 [2, 256], replicated, may hold values from 0.25 to 4
- bn_scale: float32 [2, 256], replicated, may hold values from 0.25 to 1.75
- bn_shift: float32 [2, 256], replicated, may hold values from -3 to 3
- proj_weight: bfloat16 [256, 512], replicated, may hold values from -0.375 to 0.375
- proj_bias: float32 [512], replicated, may hold values from -3 to 3
- attn_in: bfloat16 [6, 512, 512], replicated, may hold values from -0.25 to 0.25
- attn_out: bfloat16 [2, 512, 512], replicated, may hold values from -1 to 1
- ln_gain: float32 [3, 512], replicated, may hold values from 0.25 to 1.75
- ln_bias: float32 [3, 512], replicated, may hold values from -3 to 3
- ffn_in: bfloat16 [512, 1024], replicated, may hold values from -0.25 to 0.25
- ffn_in_bias: float32 [1024], replicated, may hold values from -3 to 3
- ffn_out: bfloat16 [1024, 512], replicated, may hold values from -0.1875 to 0.1875
- ffn_out_bias: float32 [512], replicated, may hold values from -3 to 3
Outputs:
- decoded: bfloat16 [2, 64, 128, 512], P(None, ('dp', 'row'))
- image_grad: float32 [2, 64, 28, 28, 256], P(None, 'dp', 'row')
- tags_grad: float32 [2, 64, 128, 512], P(None, ('dp', 'row'))
- conv_grad: float32 [2, 3, 3, 256, 256], replicated
- bn_scale_grad: float32 [2, 256], replicated
- bn_shift_grad: float32 [2, 256], replicated
- proj_grad: float32 [256, 512], replicated
- proj_bias_grad: float32 [512], replicated
- attn_in_grad: float32 [6, 512, 512], replicated
- attn_out_grad: float32 [2, 512, 512], replicated
- ln_gain_grad: float32 [3, 512], replicated
- ln_bias_grad: float32 [3, 512], replicated
- ffn_in_grad: float32 [512, 1024], replicated
- ffn_in_bias_grad: float32 [1024], replicated
- ffn_out_grad: float32 [1024, 512], replicated
- ffn_out_bias_grad: float32 [512], replicated
Inputs may be any that keep to these rules, and one draw needn't show every extreme that they name: `tag_lengths`: slot j of a table holds a tag when j is below its count; in every micro-batch some table has exactly 128.
All inputs are finite; a program needn't handle non-finite values.
Results may differ from a plain program's by a relative error of at most 0.023.
Values may be sent and summed in bfloat16 or wider, within the bound.
A program may use at most 256 MiB of HBM per device.

v0:
```python
import functools

import jax
import jax.numpy as jnp
from jax import lax
from jax.experimental import pallas as pl
from jax.experimental.pallas import tpu as pltpu
from jax.sharding import PartitionSpec as P

HEADS = 8
GROUP = 4
EPS = 1e-05
MASKED = -1e30
BF = jnp.bfloat16
F32 = jnp.float32
WIDE = 32
LEAD = 40
MIB = 1024 * 1024
MESH = pl.DeviceIdType.MESH


def dot(left, right):
    return jnp.dot(left, right, preferred_element_type=F32)


def dot_nt(left, right):
    return lax.dot_general(left, right, (((1,), (1,)), ((), ())), preferred_element_type=F32)


def dot_tn(left, right):
    return lax.dot_general(left, right, (((0,), (0,)), ((), ())), preferred_element_type=F32)


def gelu_pair(value):
    cdf = 0.5 + 0.5 * lax.erf(value * 0.7071067811865476)
    density = jnp.exp(value * value * -0.5) * 0.3989422804014327
    return value * cdf, cdf + value * density


def real_columns(rows):
    at = lax.broadcasted_iota(jnp.int32, (rows, 1), 0)
    return lax.rem(at, WIDE) < 28


def spread(shifted, held, cells):
    for b in range(3):
        shifted[WIDE : WIDE + cells, b * 256 : (b + 1) * 256] = held[
            LEAD - 1 + b : LEAD - 1 + b + cells, :
        ].astype(BF)


def three_rows(shifted, start, rows):
    return jnp.concatenate(
        [shifted[start + a * WIDE : start + a * WIDE + rows, :] for a in range(3)], axis=1
    )


def clear_edges(shifted, helds, cells):
    shifted[0:WIDE, :] = jnp.zeros((WIDE, shifted.shape[1]), BF)
    shifted[WIDE + cells :, :] = jnp.zeros((WIDE, shifted.shape[1]), BF)
    for held in helds:
        held[0:LEAD, :] = jnp.zeros((LEAD, held.shape[1]), F32)
        held[LEAD + cells :, :] = jnp.zeros((held.shape[0] - LEAD - cells, held.shape[1]), F32)


def block_forward_kernel(
    row, image, weight, mean, var, scale, shift, proj, proj_bias, key_value,
    padded, hidden, block_out, slope_one, slope_two, norm_one, norm_two, memory, cross_kv,
    shifted, held_in, held_mid, raw, loose, sent, landed, load_sem, send_sem, land_sem, home_sem,
):
    table = pl.program_id(0)
    cells = padded.shape[1]
    half = cells // 2
    tables, batches, rows = landed.shape[0], image.shape[0], sent.shape[2]
    owned = tables // batches
    group = owned * row
    me = lax.axis_index("row")
    factor = lax.rsqrt(var[...] + EPS)
    mine = pl.ds(pl.multiple_of(me * rows, WIDE), rows)

    def exchange(t, d):
        peer = lax.rem(me + d, row)
        return pltpu.make_async_remote_copy(
            src_ref=sent.at[t, peer], dst_ref=landed.at[t, mine],
            send_sem=send_sem.at[t, d - 1], recv_sem=land_sem.at[t, d - 1],
            device_id={"row": peer}, device_id_type=MESH,
        )

    def keep(t):
        return pltpu.make_async_copy(sent.at[t, me], landed.at[t, mine], home_sem.at[t])

    def take_apart(b):
        gap = jnp.zeros((WIDE - 28, 128), F32)
        for h in range(2):
            lanes = slice(h * 128, (h + 1) * 128)
            loose[h] = raw[b, :, lanes].astype(F32)
            for g in range(group):
                for r in range(rows // WIDE):
                    line = loose[h, pl.ds(r * 28 * group + g, 28, stride=group), :]
                    line = jnp.concatenate([line, gap], axis=0).astype(BF)
                    sent[b * owned + g % owned, g // owned, r * WIDE : (r + 1) * WIDE, lanes] = line

    @pl.when(table == 0)
    def _():
        loads = [pltpu.make_async_copy(image.at[b], raw.at[b], load_sem.at[b]) for b in range(batches)]
        for copy in loads:
            copy.start()
        barrier = pltpu.get_barrier_semaphore()
        for d in range(1, row):
            pl.semaphore_signal(
                barrier, inc=1, device_id={"row": lax.rem(me + d, row)}, device_id_type=MESH
            )
        for b in range(batches):
            loads[b].wait()
            take_apart(b)
            if b == 0:
                pl.semaphore_wait(barrier, row - 1)
            for t in range(b * owned, (b + 1) * owned):
                for d in range(1, row):
                    exchange(t, d).start()
                keep(t).start()
        clear_edges(shifted, (held_in, held_mid), cells)

    for d in range(1, row):
        exchange(table, d).wait_recv()
    keep(table).wait()
    padded[0] = landed[table]
    held_in[LEAD : LEAD + cells, :] = landed[table].astype(F32)
    spread(shifted, held_in, cells)
    real = real_columns(half)
    for start in (0, half):
        pre = dot(three_rows(shifted, start, half), weight[0])
        norm = (pre - mean[0:1]) * factor[0:1]
        act, slope = gelu_pair(norm * scale[0:1] + shift[0:1])
        act = jnp.where(real, act, 0.0)
        held_mid[LEAD + start : LEAD + start + half, :] = act
        hidden[0, start : start + half, :] = act.astype(BF)
        slope_one[0, start : start + half, :] = jnp.where(real, slope, 0.0).astype(BF)
        norm_one[0, start : start + half, :] = norm.astype(BF)
    spread(shifted, held_mid, cells)
    for start in (0, half):
        pre = dot(three_rows(shifted, start, half), weight[1])
        norm = (pre - mean[1:2]) * factor[1:2]
        total = norm * scale[1:2] + shift[1:2] + held_in[LEAD + start : LEAD + start + half, :]
        act, slope = gelu_pair(total)
        block = act.astype(BF)
        block_out[0, start : start + half, :] = block
        slope_two[0, start : start + half, :] = slope.astype(BF)
        norm_two[0, start : start + half, :] = norm.astype(BF)
        tokens = (dot(block, proj[...]) + proj_bias[...]).astype(BF)
        memory[0, start : start + half, :] = tokens
        for k in range(2):
            cross_kv[0, start : start + half, k * 512 : (k + 1) * 512] = dot(
                tokens, key_value[k]
            ).astype(BF)

    @pl.when(table == tables - 1)
    def _():
        for t in range(tables):
            for d in range(1, row):
                exchange(t, d).wait_send()


def whole(*shape):
    zeros = (0,) * len(shape)
    return pl.BlockSpec(shape, lambda t: zeros)


def per_table(*shape):
    zeros = (0,) * len(shape)
    return pl.BlockSpec((1,) + shape, lambda t: (t,) + zeros)


def block_forward(image, weight, mean, var, scale, shift, proj, proj_bias, attn_in, row, group, part):
    batches, width = image.shape[0], image.shape[2]
    tables, cells = batches * (group // row), part * row * WIDE
    model = proj.shape[1]
    small = jax.ShapeDtypeStruct((tables, cells, width), BF)
    stats = [whole(2, width)] * 4
    return pl.pallas_call(
        functools.partial(block_forward_kernel, row),
        grid=(tables,),
        in_specs=[pl.BlockSpec(memory_space=pl.ANY), whole(*weight.shape)] + stats
        + [whole(*proj.shape), whole(1, model), pl.BlockSpec((2,) + attn_in.shape[1:], lambda t: (2, 0, 0))],
        out_specs=[per_table(cells, width)] * 7 + [per_table(cells, model), per_table(cells, 2 * model)],
        out_shape=[small] * 7 + [
            jax.ShapeDtypeStruct((tables, cells, model), BF),
            jax.ShapeDtypeStruct((tables, cells, 2 * model), BF),
        ],
        scratch_shapes=[
            pltpu.VMEM((cells + 2 * WIDE, 3 * width), BF),
            pltpu.VMEM((cells + 80, width), F32),
            pltpu.VMEM((cells + 80, width), F32),
            pltpu.VMEM(image.shape, BF),
            pltpu.VMEM((2, image.shape[1], 128), F32),
            pltpu.VMEM((tables, row, part * WIDE, width), BF),
            pltpu.VMEM((tables, cells, width), BF),
            pltpu.SemaphoreType.DMA((batches,)),
            pltpu.SemaphoreType.DMA((tables, row - 1)),
            pltpu.SemaphoreType.DMA((tables, row - 1)),
            pltpu.SemaphoreType.DMA((tables,)),
        ],
        compiler_params=pltpu.CompilerParams(
            vmem_limit_bytes=56 * MIB, collective_id=1, has_side_effects=True
        ),
        name="block_forward",
    )(image, weight, mean, var, scale, shift, proj, proj_bias, attn_in)


def block_backward_kernel(
    grad_tokens, padded, hidden, block_out, slope_one, slope_two, norm_one, norm_two,
    weight, var, scale, proj,
    image_grad, grads, bn_sums, proj_bias_grad,
    shifted, held, kept, weight_back, conv_sum, proj_sum, bn_sum, bias_sum,
):
    step = pl.program_id(0)
    cells = padded.shape[1]
    half = cells // 2
    gain = lax.rsqrt(var[...] + EPS) * scale[...]

    @pl.when(step == 0)
    def _():
        clear_edges(shifted, (held,), cells)
        conv_sum[...] = jnp.zeros_like(conv_sum)
        proj_sum[...] = jnp.zeros_like(proj_sum)
        bn_sum[...] = jnp.zeros_like(bn_sum)
        bias_sum[...] = jnp.zeros_like(bias_sum)
        for layer in range(2):
            for tap in range(9):
                turned = weight[layer, tap * 256 : (tap + 1) * 256, :].T
                weight_back[layer, (8 - tap) * 256 : (9 - tap) * 256, :] = turned

    def add_stats(layer, grad, norm):
        bn_sum[layer : layer + 1, :] += jnp.sum(grad * norm.astype(F32), axis=0, keepdims=True)
        bn_sum[2 + layer : 3 + layer, :] += jnp.sum(grad, axis=0, keepdims=True)

    def add_conv(layer, inputs):
        turned = inputs.T
        for a in range(3):
            start = (2 - a) * WIDE
            found = dot(turned, shifted[start : start + cells, :])
            for b in range(3):
                conv_sum[layer, a, b] += found[:, (2 - b) * 256 : (3 - b) * 256]

    proj_sum[...] += dot_tn(block_out[0], grad_tokens[0])
    bias_sum[...] += jnp.sum(grad_tokens[0].astype(F32), axis=0, keepdims=True)
    for start in (0, half):
        part = slice(start, start + half)
        grad = slope_two[0, part, :].astype(F32) * dot_nt(grad_tokens[0, part, :], proj[...])
        kept[part, :] = grad
        add_stats(1, grad, norm_two[0, part, :])
        held[LEAD + start : LEAD + start + half, :] = grad * gain[1:2]
    spread(shifted, held, cells)
    for start in (0, half):
        part = slice(start, start + half)
        back = dot(three_rows(shifted, start, half), weight_back[1])
        grad = slope_one[0, part, :].astype(F32) * back
        add_stats(0, grad, norm_one[0, part, :])
        held[LEAD + start : LEAD + start + half, :] = grad * gain[0:1]
    add_conv(1, hidden[0])
    spread(shifted, held, cells)
    for start in (0, half):
        back = dot(three_rows(shifted, start, half), weight_back[0]) + kept[start : start + half, :]
        image_grad[0, start : start + half, :] = back.astype(BF)
    add_conv(0, padded[0])

    @pl.when(step == pl.num_programs(0) - 1)
    def _():
        for a in range(3):
            for b in range(3):
                rows = slice((3 * a + b) * 256, (3 * a + b + 1) * 256)
                for layer in range(2):
                    grads[rows, layer * 256 : (layer + 1) * 256] = conv_sum[layer, a, b].astype(BF)
        grads[9 * 256 :, :] = proj_sum[...].astype(BF)
        bn_sums[...] = bn_sum[...]
        proj_bias_grad[...] = bias_sum[...]


def block_backward(
    grad_tokens, padded, hidden, block_out, slope_one, slope_two, norm_one, norm_two,
    weight, var, scale, proj,
):
    tables, cells, model = grad_tokens.shape
    width = proj.shape[0]
    per = per_table(cells, width)
    conv_shape = (2, 3, 3, width, width)
    return pl.pallas_call(
        block_backward_kernel,
        grid=(tables,),
        in_specs=[per_table(cells, model)] + [per] * 7
        + [whole(*weight.shape)] + [whole(2, width)] * 2 + [whole(*proj.shape)],
        out_specs=[
            per, whole(10 * width, model), whole(4, width), whole(1, model),
        ],
        out_shape=[
            jax.ShapeDtypeStruct((tables, cells, width), BF),
            jax.ShapeDtypeStruct((10 * width, model), BF),
            jax.ShapeDtypeStruct((4, width), F32),
            jax.ShapeDtypeStruct((1, model), F32),
        ],
        scratch_shapes=[
            pltpu.VMEM((cells + 2 * WIDE, 3 * width), BF),
            pltpu.VMEM((cells + 80, width), F32),
            pltpu.VMEM((cells, width), F32),
            pltpu.VMEM(weight.shape, BF),
            pltpu.VMEM(conv_shape, F32),
            pltpu.VMEM(proj.shape, F32),
            pltpu.VMEM((4, width), F32),
            pltpu.VMEM((1, model), F32),
        ],
        compiler_params=pltpu.CompilerParams(vmem_limit_bytes=56 * MIB),
        name="block_backward",
    )(
        grad_tokens, padded, hidden, block_out, slope_one, slope_two, norm_one, norm_two,
        weight, var, scale, proj,
    )


def lane_masks(rows, lanes):
    at = lax.broadcasted_iota(jnp.int32, (rows, lanes), 1) // 64
    return [at == h for h in range(GROUP)]


def by_head(value, masks):
    zero = jnp.zeros_like(value)
    return jnp.concatenate([jnp.where(m, value, zero) for m in masks], axis=0)


def own_lanes(stacked, masks):
    rows = stacked.shape[0] // GROUP
    total = stacked[0:rows]
    for h in range(1, GROUP):
        total = jnp.where(masks[h], stacked[h * rows : (h + 1) * rows], total)
    return total


def softmax_rows(scores):
    raised = jnp.exp(scores - jnp.max(scores, axis=-1, keepdims=True))
    return raised * (1.0 / jnp.sum(raised, axis=-1, keepdims=True))


def normalise(value):
    center = value - jnp.mean(value, axis=-1, keepdims=True)
    inverse = lax.rsqrt(jnp.mean(center * center, axis=-1, keepdims=True) + EPS)
    return center * inverse, inverse


def norm_back(upstream, gain, unit, inverse):
    scaled = upstream * gain
    mean = jnp.mean(scaled, axis=-1, keepdims=True)
    along = jnp.mean(scaled * unit, axis=-1, keepdims=True)
    return inverse * (scaled - mean - unit * along)


def column_sum(value):
    return jnp.sum(value, axis=0, keepdims=True)


def decoder_kernel(
    lengths, ln_gain, ln_bias, ffn_in_bias, ffn_out_bias,
    tags_far, cotangent_far, memory_far, cross_kv_far, attn_in_far, attn_out_far, ffn_in_far, ffn_out_far,
    decoded, tags_grad, grad_tokens, grads_far,
    ln_gain_grad, ln_bias_grad, ffn_in_bias_grad, ffn_out_bias_grad,
    tags, cotangent, memory, cross_kv, attn_in, attn_out, ffn_in, ffn_out,
    qkv, mix, self_shares, cross_shares, cross_q, up, grad_qkv, grad_q, grad_kv, pair_sum,
    staged, weight_sem, kv_sem, memory_sem, staged_sem,
    grads, grad_sem,
):
    tables, cells = memory_far.shape[0], memory_far.shape[1]
    slots = tags.shape[0] // tables

    def fetch_kv(t):
        return pltpu.make_async_copy(cross_kv_far.at[t], cross_kv.at[t], kv_sem.at[t])

    def fetch_memory(t):
        slot = lax.rem(t, 2)
        return pltpu.make_async_copy(memory_far.at[t], memory.at[slot], memory_sem.at[slot])

    def put_tokens(t):
        slot = lax.rem(t, 2)
        return pltpu.make_async_copy(staged.at[slot], grad_tokens.at[t], staged_sem.at[slot])

    fetches = [
        pltpu.make_async_copy(far, near, weight_sem.at[i])
        for i, (far, near) in enumerate(
            [(tags_far, tags)]
            + [(attn_in_far.at[k], attn_in.at[k]) for k in range(4)]
            + [(attn_out_far, attn_out), (cotangent_far, cotangent)]
            + [(ffn_in_far, ffn_in), (ffn_out_far, ffn_out)]
            + [(attn_in_far.at[k], attn_in.at[k]) for k in (4, 5)]
        )
    ]
    for copy in fetches[:6]:
        copy.start()
    for t in range(tables):
        fetch_kv(t).start()
    for copy in fetches[6:]:
        copy.start()
    fetch_memory(0).start()
    half = 256
    wide_f32 = lane_masks(slots, half)
    real_key = lax.rem(lax.broadcasted_iota(jnp.int32, (GROUP * slots, cells), 1), WIDE) < 28

    def allowed_of(t):
        row = lax.broadcasted_iota(jnp.int32, (slots, slots), 0)
        col = lax.broadcasted_iota(jnp.int32, (slots, slots), 1)
        once = (col <= row) & (col < lengths[t])
        return jnp.concatenate([once] * GROUP, axis=0)

    def put_grad(i, value):
        grads[i] = value.astype(BF)
        copy = pltpu.make_async_copy(grads.at[i], grads_far.at[i], grad_sem.at[i])
        copy.start()
        puts.append(copy)

    puts = []
    fetches[0].wait()
    for k in range(3):
        fetches[1 + k].wait()
        qkv[k] = dot(tags[...], attn_in[k]).astype(BF)

    def self_forward(t, carry):
        rows = pl.ds(pl.multiple_of(t * slots, slots), slots)
        allowed = allowed_of(t)
        for g in range(2):
            lanes = slice(g * half, (g + 1) * half)
            query = by_head(qkv[0, rows, lanes], wide_f32)
            scores = dot_nt(query, qkv[1, rows, lanes]) * 0.125
            shares = softmax_rows(jnp.where(allowed, scores, MASKED)).astype(BF)
            self_shares[t, g] = shares
            mix[0, rows, lanes] = own_lanes(dot(shares, qkv[2, rows, lanes]), wide_f32).astype(BF)
        return carry

    lax.fori_loop(0, tables, self_forward, 0)
    fetches[5].wait()
    first_unit, first_inv = normalise(tags[...].astype(F32) + dot(mix[0], attn_out[0]))
    first = first_unit * ln_gain[0:1] + ln_bias[0:1]
    first_low = first.astype(BF)
    fetches[4].wait()
    cross_q[...] = dot(first_low, attn_in[3]).astype(BF)

    def cross_forward(t, carry):
        fetch_kv(t).wait()
        rows = pl.ds(pl.multiple_of(t * slots, slots), slots)
        for g in range(2):
            lanes = slice(g * half, (g + 1) * half)
            query = by_head(cross_q[rows, lanes], wide_f32)
            scores = dot_nt(query, cross_kv[t, :, lanes]) * 0.125
            shares = softmax_rows(jnp.where(real_key, scores, MASKED)).astype(BF)
            cross_shares[t, g] = shares
            value = cross_kv[t, :, 512 + g * half : 512 + (g + 1) * half]
            mix[1, rows, lanes] = own_lanes(dot(shares, value), wide_f32).astype(BF)
        return carry

    lax.fori_loop(0, tables, cross_forward, 0)
    second_unit, second_inv = normalise(first + dot(mix[1], attn_out[1]))
    second = second_unit * ln_gain[1:2] + ln_bias[1:2]
    second_low = second.astype(BF)
    for copy in fetches[6:]:
        copy.wait()
    act, slope = gelu_pair(dot(second_low, ffn_in[...]) + ffn_in_bias[...])
    inner_act = act.astype(BF)
    third_unit, third_inv = normalise(second + dot(inner_act, ffn_out[...]) + ffn_out_bias[...])
    decoded[...] = (third_unit * ln_gain[2:3] + ln_bias[2:3]).astype(BF)

    up_three = cotangent[...].astype(F32)
    ln_gain_grad[2:3, :] = column_sum(up_three * third_unit)
    ln_bias_grad[2:3, :] = column_sum(up_three)
    grad_third = norm_back(up_three, ln_gain[2:3], third_unit, third_inv)
    grad_outer = grad_third.astype(BF)
    ffn_out_total = dot_tn(inner_act, grad_outer)
    for k in range(2):
        put_grad(8 + k, ffn_out_total[k * 512 : (k + 1) * 512])
    ffn_out_bias_grad[...] = column_sum(grad_outer.astype(F32))
    grad_inner = (slope * dot_nt(grad_outer, ffn_out[...])).astype(BF)
    ffn_in_total = dot_tn(second_low, grad_inner)
    for k in range(2):
        put_grad(10 + k, ffn_in_total[:, k * 512 : (k + 1) * 512])
    ffn_in_bias_grad[...] = column_sum(grad_inner.astype(F32))
    up_two = grad_third + dot_nt(grad_inner, ffn_in[...])
    ln_gain_grad[1:2, :] = column_sum(up_two * second_unit)
    ln_bias_grad[1:2, :] = column_sum(up_two)
    grad_second = norm_back(up_two, ln_gain[1:2], second_unit, second_inv)
    grad_cross_out = grad_second.astype(BF)
    put_grad(7, dot_tn(mix[1], grad_cross_out))
    up[...] = dot_nt(grad_cross_out, attn_out[1]).astype(BF)
    pair_sum[...] = jnp.zeros_like(pair_sum)

    def cross_back(t, carry):
        @pl.when(t + 1 < tables)
        def _():
            fetch_memory(t + 1).start()

        rows = pl.ds(pl.multiple_of(t * slots, slots), slots)
        for g in range(2):
            lanes = slice(g * half, (g + 1) * half)
            value_lanes = slice(512 + g * half, 512 + (g + 1) * half)
            query = by_head(cross_q[rows, lanes], wide_f32)
            upstream = by_head(up[rows, lanes], wide_f32)
            low = cross_shares[t, g]
            shares = low.astype(F32)
            grad_shares = dot_nt(upstream, cross_kv[t, :, value_lanes])
            mean = jnp.sum(grad_shares * shares, axis=-1, keepdims=True)
            grad_scores = (shares * (grad_shares - mean)).astype(BF)
            grad_q[rows, lanes] = (
                own_lanes(dot(grad_scores, cross_kv[t, :, lanes]), wide_f32) * 0.125
            ).astype(BF)
            grad_kv[:, lanes] = (dot_tn(grad_scores, query) * 0.125).astype(BF)
            grad_kv[:, value_lanes] = dot_tn(low, upstream).astype(BF)
        @pl.when(t >= 2)
        def _():
            put_tokens(t - 2).wait()

        slot = lax.rem(t, 2)
        staged[slot] = (
            dot_nt(grad_kv[:, 0:512], attn_in[4]) + dot_nt(grad_kv[:, 512:1024], attn_in[5])
        ).astype(BF)
        put_tokens(t).start()
        fetch_memory(t).wait()
        pair_sum[...] += dot_tn(memory[slot], grad_kv[...])
        return carry

    lax.fori_loop(0, tables, cross_back, 0)
    for t in range(max(tables - 2, 0), tables):
        put_tokens(t).wait()
    for k in range(2):
        put_grad(4 + k, pair_sum[:, k * 512 : (k + 1) * 512])
    put_grad(3, dot_tn(first_low, grad_q[...]))
    up_one = grad_second + dot_nt(grad_q[...], attn_in[3])
    ln_gain_grad[0:1, :] = column_sum(up_one * first_unit)
    ln_bias_grad[0:1, :] = column_sum(up_one)
    grad_first = norm_back(up_one, ln_gain[0:1], first_unit, first_inv)
    grad_self_out = grad_first.astype(BF)
    put_grad(6, dot_tn(mix[0], grad_self_out))
    up[...] = dot_nt(grad_self_out, attn_out[0]).astype(BF)

    def self_back(t, carry):
        rows = pl.ds(pl.multiple_of(t * slots, slots), slots)
        for g in range(2):
            lanes = slice(g * half, (g + 1) * half)
            query = by_head(qkv[0, rows, lanes], wide_f32)
            upstream = by_head(up[rows, lanes], wide_f32)
            low = self_shares[t, g]
            shares = low.astype(F32)
            grad_shares = dot_nt(upstream, qkv[2, rows, lanes])
            mean = jnp.sum(grad_shares * shares, axis=-1, keepdims=True)
            grad_scores = (shares * (grad_shares - mean)).astype(BF)
            grad_qkv[0, rows, lanes] = (
                own_lanes(dot(grad_scores, qkv[1, rows, lanes]), wide_f32) * 0.125
            ).astype(BF)
            grad_qkv[1, rows, lanes] = (dot_tn(grad_scores, query) * 0.125).astype(BF)
            grad_qkv[2, rows, lanes] = dot_tn(low, upstream).astype(BF)
        return carry

    lax.fori_loop(0, tables, self_back, 0)
    total = grad_first
    for k in range(3):
        put_grad(k, dot_tn(tags[...], grad_qkv[k]))
        total = total + dot_nt(grad_qkv[k], attn_in[k])
    tags_grad[...] = total
    for copy in puts:
        copy.wait()


def decoder(
    lengths, tags, cotangent, memory, cross_kv, attn_in, attn_out, ln_gain, ln_bias,
    ffn_in, ffn_in_bias, ffn_out, ffn_out_bias,
):
    tables, cells, model = memory.shape
    rows = tags.shape[0]
    slots = rows // tables
    inner = ffn_in.shape[1]
    here = pl.BlockSpec(memory_space=pltpu.VMEM)
    far = pl.BlockSpec(memory_space=pl.ANY)
    shape = jax.ShapeDtypeStruct
    stacked = GROUP * slots
    return pl.pallas_call(
        decoder_kernel,
        in_specs=[pl.BlockSpec(memory_space=pltpu.SMEM)] + [here] * 4 + [far] * 8,
        out_specs=[here] * 2 + [far] * 2 + [here] * 4,
        out_shape=[
            shape((rows, model), BF), shape((rows, model), F32), shape((tables, cells, model), BF),
            shape((12, 512, model), BF), shape((3, model), F32), shape((3, model), F32),
            shape((1, inner), F32), shape((1, model), F32),
        ],
        scratch_shapes=[
            pltpu.VMEM((rows, model), BF),
            pltpu.VMEM((rows, model), BF),
            pltpu.VMEM((2, cells, model), BF),
            pltpu.VMEM((tables, cells, 2 * model), BF),
            pltpu.VMEM(attn_in.shape, BF),
            pltpu.VMEM(attn_out.shape, BF),
            pltpu.VMEM(ffn_in.shape, BF),
            pltpu.VMEM(ffn_out.shape, BF),
            pltpu.VMEM((3, rows, model), BF),
            pltpu.VMEM((2, rows, model), BF),
            pltpu.VMEM((tables, 2, stacked, slots), BF),
            pltpu.VMEM((tables, 2, stacked, cells), BF),
            pltpu.VMEM((rows, model), BF),
            pltpu.VMEM((rows, model), BF),
            pltpu.VMEM((3, rows, model), BF),
            pltpu.VMEM((rows, model), BF),
            pltpu.VMEM((cells, 2 * model), BF),
            pltpu.VMEM((model, 2 * model), F32),
            pltpu.VMEM((2, cells, model), BF),
            pltpu.SemaphoreType.DMA((11,)),
            pltpu.SemaphoreType.DMA((tables,)),
            pltpu.SemaphoreType.DMA((2,)),
            pltpu.SemaphoreType.DMA((2,)),
            pltpu.VMEM((12, 512, model), BF),
            pltpu.SemaphoreType.DMA((12,)),
        ],
        compiler_params=pltpu.CompilerParams(vmem_limit_bytes=60 * MIB),
        name="decoder",
    )(
        lengths, ln_gain, ln_bias, ffn_in_bias, ffn_out_bias,
        tags, cotangent, memory, cross_kv, attn_in, attn_out, ffn_in, ffn_out,
    )


def orders(dp, row):
    row_bits = [("row", 1 << i) for i in range(row.bit_length() - 1)]
    dp_bits = [("dp", 1 << i) for i in range(dp.bit_length() - 1)]
    pair, others = row_bits[:1], row_bits[1:]
    near, far = dp_bits[:1], dp_bits[1:]
    return [pair + near + others + far, pair + others + near + far, pair + far + near + others]


def plan_of(units):
    turn = (0, 2, 1) * 4 + (0, 2, 0, 0, 0)
    return [(turn[i % len(turn)], i, 1) for i in range(units)]


def side_of(axis, bit):
    return lax.rem(lax.axis_index(axis) // bit, 2)


def partner_of(axis, bit):
    return {axis: lax.axis_index(axis) + bit * (1 - 2 * side_of(axis, bit))}


def add_rows(target, held, start, landed, at, rows):
    step = 128
    while rows % step:
        step //= 2

    def one(i, carry):
        here = pl.ds(pl.multiple_of(start + i * step, 16), step)
        there = pl.ds(pl.multiple_of(at + i * step, 16), step)
        target[here, :] = held[here, :] + landed[there, :]
        return carry

    lax.fori_loop(0, rows // step, one, 0)


def reduce_kernel(plan, streams, unit, sizes, row, *refs):
    count = len(sizes)
    parts, image_grad, smalls, refs = refs[:count], refs[count], refs[count + 1 : count + 7], refs[count + 7 :]
    total, small_total, image_back = refs[:3]
    held, landed, done, small_held, small_landed = refs[3:8]
    load_sem, send_sem, land_sem, back_sem, home_sem = refs[8:13]
    small_send, small_land, out_sem, image_send, image_land, image_sem = refs[13:]
    stages = len(streams[0])
    rows_all = sum(sizes)
    bounds = [sum(sizes[:i]) for i in range(count + 1)]
    loads = [
        pltpu.make_async_copy(part, held.at[pl.ds(bounds[i], sizes[i]), :], load_sem.at[i])
        for i, part in enumerate(parts)
    ]
    for copy in loads:
        copy.start()
    barrier = pltpu.get_barrier_semaphore()
    me = lax.axis_index("row")
    peers = [{"row": lax.rem(me + d, row)} for d in range(1, row)]
    across = [partner_of(axis, bit) for axis, bit in streams[0] if axis == "dp"]
    for device in peers + across:
        pl.semaphore_signal(barrier, inc=1, device_id=device, device_id_type=MESH)
    pl.semaphore_wait(barrier, len(peers) + len(across))
    owned, rows = image_back.shape[1] // row, image_back.shape[2]
    images = []
    for t in range(image_grad.shape[0]):
        target = image_back.at[t // owned, me * owned + t % owned]
        for d in range(1, row):
            peer = lax.rem(me + d, row)
            images.append(pltpu.make_async_remote_copy(
                src_ref=image_grad.at[t, pl.ds(pl.multiple_of(peer * rows, WIDE), rows)], dst_ref=target,
                send_sem=image_send.at[t, d - 1], recv_sem=image_land.at[t, d - 1],
                device_id={"row": peer}, device_id_type=MESH,
            ))
        images.append(pltpu.make_async_copy(
            image_grad.at[t, pl.ds(pl.multiple_of(me * rows, WIDE), rows)], target, image_sem.at[t],
        ))
    for copy in images:
        copy.start()
    bn, proj_bias, gain, bias, ffn_in_bias, ffn_out_bias = smalls
    small_held[0] = jnp.concatenate([
        jnp.concatenate([bn[0:2, :], bn[2:4, :]], axis=1), proj_bias[...], ffn_out_bias[...],
        ffn_in_bias[:, 0:512], ffn_in_bias[:, 512:1024], jnp.zeros((2, 512), F32),
        gain[...], bias[...], jnp.zeros((2, 512), F32),
    ], axis=0)
    loaded = [False] * count

    def need(first, last):
        for i in range(count):
            if bounds[i] < last and bounds[i + 1] > first and not loaded[i]:
                loads[i].wait()
                loaded[i] = True

    state = [dict(start=first * unit, rows=n * unit, at=0) for _, first, n in plan]
    flights, backs, outs = {}, {}, []

    def small_step(s):
        if s > 0:
            flights["small", s - 1].wait()
            both = small_held[s - 1] + small_landed[s - 1]
            if s == stages:
                small_total[...] = both
                return
            small_held[s] = both
        axis, bit = streams[0][s]
        copy = pltpu.make_async_remote_copy(
            src_ref=small_held.at[s], dst_ref=small_landed.at[s],
            send_sem=small_send.at[s], recv_sem=small_land.at[s],
            device_id=partner_of(axis, bit), device_id_type=MESH,
        )
        copy.start()
        flights["small", s] = copy

    def collect(c, s, target):
        _, first, n = plan[c]
        now = state[c]
        flights[c, s].wait_recv()
        add_rows(target, held, now["start"], landed, first * unit + now["at"], now["rows"])
        now["at"] += now["rows"]

    def split(c, s):
        stream, first, n = plan[c]
        now = state[c]
        axis, bit = streams[stream][s]
        if s == 0:
            need(first * unit, (first + n) * unit)
        else:
            collect(c, s - 1, held)
        half = now["rows"] // 2
        side = side_of(axis, bit)
        base = now["start"]
        copy = pltpu.make_async_remote_copy(
            src_ref=held.at[pl.ds(pl.multiple_of(base + (1 - side) * half, 16), half), :],
            dst_ref=landed.at[pl.ds(first * unit + now["at"], half), :],
            send_sem=send_sem.at[c, s], recv_sem=land_sem.at[c, s],
            device_id=partner_of(axis, bit), device_id_type=MESH,
        )
        copy.start()
        flights[c, s] = copy
        now["start"] = base + side * half
        now["rows"] = half

    def merge(c, s):
        stream, first, n = plan[c]
        now = state[c]
        axis, bit = streams[stream][s]
        if s == stages - 1:
            collect(c, s, done)
        else:
            backs[c, s + 1].wait_recv()
            now["rows"] *= 2
            now["start"] = now["start"] - side_of(*streams[stream][s + 1]) * (now["rows"] // 2)
        region = done.at[pl.ds(pl.multiple_of(now["start"], 16), now["rows"]), :]
        copy = pltpu.make_async_remote_copy(
            src_ref=region, dst_ref=region,
            send_sem=back_sem.at[c, s], recv_sem=home_sem.at[c, s],
            device_id=partner_of(axis, bit), device_id_type=MESH,
        )
        copy.start()
        backs[c, s] = copy

    def finish(c):
        _, first, n = plan[c]
        backs[c, 0].wait_recv()
        last = min((first + n) * unit, rows_all)
        if last > first * unit:
            region = pl.ds(first * unit, last - first * unit)
            copy = pltpu.make_async_copy(done.at[region, :], total.at[region, :], out_sem.at[c])
            copy.start()
            outs.append(copy)

    lags, seen = [], {}
    for stream, _, _ in plan:
        lags.append(seen.get(stream, 0))
        seen[stream] = lags[-1] + 1
    for turn in range(2 * stages + 1 + max(lags)):
        if turn <= stages:
            small_step(turn)
        for c, lag in reversed(list(enumerate(lags))):
            k = turn - lag
            if 0 <= k < stages:
                split(c, k)
            elif stages <= k < 2 * stages:
                merge(c, 2 * stages - 1 - k)
            elif k == 2 * stages:
                finish(c)
    for c in range(len(plan)):
        for s in range(stages):
            flights[c, s].wait_send()
            backs[c, s].wait_send()
    for copy in outs + images:
        copy.wait()


def reduce_all(parts, image_grad, smalls, dp, row, batches):
    streams = orders(dp, row)
    stages = len(streams[0])
    sizes = [p.shape[0] for p in parts]
    rows, width = sum(sizes), parts[0].shape[1]
    unit = 16 * dp * row
    plan = plan_of(-(-rows // unit))
    chunks = len(plan)
    tables, cells, channels = image_grad.shape
    back = (batches, tables // batches * row, cells // row, channels)
    small = (16, width)
    far = pl.BlockSpec(memory_space=pl.ANY)
    near = pl.BlockSpec(memory_space=pltpu.VMEM)
    sem = pltpu.SemaphoreType.DMA
    return pl.pallas_call(
        functools.partial(reduce_kernel, plan, streams, unit, sizes, row),
        in_specs=[far] * (len(parts) + 1) + [near] * len(smalls),
        out_specs=[far, near, far],
        out_shape=[
            jax.ShapeDtypeStruct((rows, width), BF),
            jax.ShapeDtypeStruct(small, F32),
            jax.ShapeDtypeStruct(back, BF),
        ],
        scratch_shapes=[
            pltpu.VMEM((chunks * unit, width), BF),
            pltpu.VMEM((chunks * unit, width), BF),
            pltpu.VMEM((chunks * unit, width), BF),
            pltpu.VMEM((stages,) + small, F32),
            pltpu.VMEM((stages,) + small, F32),
            sem((len(parts),)), sem((chunks, stages)), sem((chunks, stages)),
            sem((chunks, stages)), sem((chunks, stages)),
            sem((stages,)), sem((stages,)), sem((chunks,)),
            sem((tables, row - 1)), sem((tables, row - 1)), sem((tables,)),
        ],
        compiler_params=pltpu.CompilerParams(
            vmem_limit_bytes=60 * MIB, collective_id=0, has_side_effects=True
        ),
        name="reduce_all",
    )(*parts, image_grad, *smalls)


def widen_kernel(
    small, total, back, conv, proj, attn_in, attn_out, ffn_in, ffn_out, image_grad,
    bn_scale, bn_shift, proj_bias, gain, bias, ffn_in_bias, ffn_out_bias,
    narrow, wide, narrow_image, wide_image, in_sem, out_sem, image_in, image_out,
):
    units = in_sem.shape[0]
    batches, group = back.shape[0], back.shape[1]

    def rows(i):
        return pl.ds(i * 512, 512)

    fetches = [
        pltpu.make_async_copy(total.at[rows(i)], narrow.at[rows(i)], in_sem.at[i]) for i in range(units)
    ]
    images = [(b, g) for b in range(batches) for g in range(group)]
    image_fetches = [
        pltpu.make_async_copy(back.at[b, g], narrow_image.at[i], image_in.at[i])
        for i, (b, g) in enumerate(images)
    ]
    for copy in fetches + image_fetches:
        copy.start()
    bn_scale[...] = small[0:2, 0:256]
    bn_shift[...] = small[0:2, 256:512]
    proj_bias[...] = small[2:3, :]
    ffn_out_bias[...] = small[3:4, :]
    ffn_in_bias[:, 0:512] = small[4:5, :]
    ffn_in_bias[:, 512:1024] = small[5:6, :]
    gain[...] = small[8:11, :]
    bias[...] = small[11:14, :]
    slots = wide.shape[0]
    targets = [attn_in.at[i] for i in range(6)] + [attn_out.at[i] for i in range(2)]
    targets += [ffn_out.at[rows(i)] for i in range(2)]
    targets += [ffn_in.at[:, pl.ds(i * 512, 512)] for i in range(2)]
    pending = []

    def put(i, pairs):
        copies = [
            pltpu.make_async_copy(source, target, out_sem.at[i % slots, j])
            for j, (source, target) in enumerate(pairs)
        ]
        for copy in copies:
            copy.start()
        pending.append(copies)

    for i in range(units):
        fetches[i].wait()
        if i >= slots:
            for copy in pending[i - slots]:
                copy.wait()
        slot = wide.at[i % slots]
        slot[...] = narrow[rows(i), :].astype(F32)
        if i < 12:
            put(i, [(slot, targets[i])])
            continue
        pairs = []
        for half in range(2):
            tap = 2 * (i - 12) + half
            here = pl.ds(half * 256, 256)
            if tap < 9:
                for layer in range(2):
                    lanes = pl.ds(layer * 256, 256)
                    pairs.append((slot.at[here, lanes], conv.at[layer, tap // 3, tap % 3]))
            else:
                pairs.append((slot.at[here], proj))
        put(i, pairs)
    waits = []
    for b in range(batches):
        for g in range(group):
            image_fetches[b * group + g].wait()
            for r in range(back.shape[2] // WIDE):
                line = narrow_image[b * group + g, r * WIDE : (r + 1) * WIDE, :].astype(F32)
                for h in range(2):
                    lanes = slice(h * 128, (h + 1) * 128)
                    wide_image[b, h, pl.ds(r * 28 * group + g, 28, stride=group), :] = line[0:28, lanes]
        for h in range(2):
            waits.append(pltpu.make_async_copy(
                wide_image.at[b, h], image_grad.at[b, :, pl.ds(h * 128, 128)], image_out.at[b, h]
            ))
            waits[-1].start()
    for copies in pending[-slots:] + [waits]:
        for copy in copies:
            copy.wait()


def widen(small, total, back, image_shape, width, model, inner):
    rows = total.shape[0]
    units = rows // 512
    batches, group = back.shape[:2]
    far = pl.BlockSpec(memory_space=pl.ANY)
    near = pl.BlockSpec(memory_space=pltpu.VMEM)
    sem = pltpu.SemaphoreType.DMA
    shapes = [
        (2, 3, 3, width, width), (width, model), (6, model, model), (2, model, model),
        (model, inner), (inner, model), image_shape,
    ]
    small_shapes = [(2, width)] * 2 + [(1, model), (3, model), (3, model), (1, inner), (1, model)]
    return pl.pallas_call(
        widen_kernel,
        in_specs=[near] + [far] * 2,
        out_specs=[far] * 7 + [near] * 7,
        out_shape=[jax.ShapeDtypeStruct(s, F32) for s in shapes + small_shapes],
        scratch_shapes=[
            pltpu.VMEM((rows, model), BF),
            pltpu.VMEM((4, 512, model), F32),
            pltpu.VMEM((batches * group,) + back.shape[2:], BF),
            pltpu.VMEM((batches, 2, image_shape[1], 128), F32),
            sem((units,)), sem((4, 4)), sem((batches * group,)), sem((batches, 2)),
        ],
        compiler_params=pltpu.CompilerParams(vmem_limit_bytes=60 * MIB),
        name="widen",
    )(small, total, back)


def body(
    image, tags, tag_lengths, cotangent, conv_weight, bn_mean, bn_var, bn_scale, bn_shift,
    proj_weight, proj_bias, attn_in, attn_out, ln_gain, ln_bias,
    ffn_in, ffn_in_bias, ffn_out, ffn_out_bias,
):
    batches, owned, slots, model = tags.shape
    width = image.shape[-1]
    tables = batches * owned
    row = lax.axis_size("row")
    group, part, breadth = image.shape[1:4]
    flat_image = image.transpose(0, 2, 3, 1, 4).reshape(batches, part * breadth * group, width)
    weight = conv_weight.reshape(2, 9 * width, width)
    forward = block_forward(
        flat_image, weight, bn_mean, bn_var, bn_scale, bn_shift,
        proj_weight, proj_bias.reshape(1, -1), attn_in, row, group, part,
    )
    padded, hidden, block_out, slope_one, slope_two, norm_one, norm_two, memory, cross_kv = forward
    decoded, tags_grad, grad_tokens, decoder_g, gain_g, bias_g, ffn_in_bias_g, ffn_out_bias_g = decoder(
        tag_lengths.reshape(-1), tags.reshape(-1, model), cotangent.reshape(-1, model),
        memory, cross_kv, attn_in, attn_out, ln_gain, ln_bias,
        ffn_in, ffn_in_bias.reshape(1, -1), ffn_out, ffn_out_bias.reshape(1, -1),
    )
    image_grad, block_g, bn_g, proj_bias_g = block_backward(
        grad_tokens, padded, hidden, block_out, slope_one, slope_two, norm_one, norm_two,
        weight, bn_var, bn_scale, proj_weight,
    )
    total, small, back = reduce_all(
        (decoder_g.reshape(-1, model), block_g), image_grad,
        (bn_g, proj_bias_g, gain_g, bias_g, ffn_in_bias_g, ffn_out_bias_g),
        lax.axis_size("dp"), row, batches,
    )
    (
        conv_g, proj_g, attn_in_g, attn_out_g, ffn_in_g, ffn_out_g, image_g,
        bn_scale_g, bn_shift_g, proj_bias_g, gain_g, bias_g, ffn_in_bias_g, ffn_out_bias_g,
    ) = widen(small, total, back, flat_image.shape, width, model, ffn_in.shape[1])
    image_g = image_g.reshape(batches, part, breadth, group, width).transpose(0, 3, 1, 2, 4)
    return (
        decoded.reshape(tags.shape), image_g, tags_grad.reshape(tags.shape),
        conv_g, bn_scale_g, bn_shift_g, proj_g, proj_bias_g.reshape(-1),
        attn_in_g, attn_out_g, gain_g, bias_g,
        ffn_in_g, ffn_in_bias_g.reshape(-1), ffn_out_g, ffn_out_bias_g.reshape(-1),
    )


def solution(mesh):
    by_rows = P(None, "dp", "row", None, None)
    by_table = P(None, ("dp", "row"), None, None)
    return jax.shard_map(
        body,
        mesh=mesh,
        in_specs=(by_rows, by_table, P(None, ("dp", "row")), by_table) + (P(),) * 15,
        out_specs=(by_table, by_rows, by_table) + (P(),) * 13,
        check_vma=False,
    )
```

profile of v0, /device:TPU:1, one launch (start us, length us, event | category | flops | bytes accessed | tf_op | source)
XLA Modules:
  0.0 246.8 jit_solution(12930540052153464440)
XLA Ops:
  0.6 1.3 reshape.77.lengths
  1.9 35.7 %block_forward.1 = (bf16[4,896,256]{2,1,0:T(8,128)(2,1)}, bf16[4,896,256]{2,1,0:T(8,128)(2,1)}, bf16[4,896,256]{2,1,0:T(8,128)(2,1)}, bf16[4,896,256]{2,1,0:T(8,...) custom-call(bf16[2,1568,256]{2,1,0:T(8,128)(2,1)} %bitcast.21, ...), custom_call_target="tpu_custom_call" | custom-call | tf_op jit(solution)/shard_map/block_forward/pallas_call | solution.py:180
  37.6 56.7 %decoder.1 = (bf16[512,512]{1,0:T(8,128)(2,1)}, f32[512,512]{1,0:T(8,128)}, bf16[4,896,512]{2,1,0:T(8,128)(2,1)}, bf16[12,512,512]{2,1,0:T(8,128)(2,1)}, f32[3,5...) custom-call(s32[4]{0:T(128)} %reshape.77.lengths, f32[3,512]{1,0:T(4,128)} %ln_gain.1, ...), custom_call_target="tpu_custom_call" | custom-call | tf_op jit(solution)/shard_map/decoder/pallas_call | solution.py:577
  94.3 29.9 %block_backward.1 = (bf16[4,896,256]{2,1,0:T(8,128)(2,1)}, bf16[2560,512]{1,0:T(8,128)(2,1)}, f32[4,256]{1,0:T(4,128)}, f32[1,512]{1,0:T(1,128)}) custom-call(bf16[4,896,512]{2,1,0:T(8,128)(2,1)} %get-tuple-element.58.grad_tokens, bf16[4,896,256]{2,1,0:T(8,128)(2,1)} %get-tuple-element.59.padded, bf16[4,896,256]{2,1,0:T(8,128)(2,1)} %get-tuple-element.60.hidden, ...), custom_call_target="tpu_custom_call" | custom-call | tf_op jit(solution)/shard_map/block_backward/pallas_call | solution.py:287
  124.3 109.6 %reduce_all.1 = (bf16[8704,512]{1,0:T(8,128)(2,1)}, f32[16,512]{1,0:T(8,128)}, bf16[2,8,224,256]{3,2,1,0:T(8,128)(2,1)}) custom-call(bf16[6144,512]{1,0:T(8,128)(2,1)} %bitcast.20, bf16[2560,512]{1,0:T(8,128)(2,1)} %get-tuple-element.66.refs_1_, bf16[4,896,256]{2,1,0:T(8,128)(2,1)} %get-tuple-element.67.refs_2_, f32[4,256]{1,0:T(4,128)} %get-tuple-element.68.refs_3_, ...), custom_call_target="tpu_custom_call" | custom-call | tf_op jit(solution)/shard_map/reduce_all/pallas_call | solution.py:824
  233.9 12.7 %widen.1 = (f32[2,3,3,256,256]{4,3,2,1,0:T(8,128)}, f32[256,512]{1,0:T(8,128)}, f32[6,512,512]{2,1,0:T(8,128)}, f32[2,512,512]{2,1,0:T(8,128)}, f32[512,1024]{1,...) custom-call(f32[16,512]{1,0:T(8,128)} %get-tuple-element.74.small, ...), custom_call_target="tpu_custom_call" | custom-call | tf_op jit(solution)/shard_map/widen/pallas_call | solution.py:947
where the time goes:
time: 247 us
  Pallas kernels  245 us (99%)
    pallas_call x1, Pallas kernels, reduce_all(): pl.pallas_call(functools.partial(reduce_kernel, plan, streams, unit, size...  110 us
    pallas_call x1, Pallas kernels, decoder(): pl.pallas_call(decoder_kernel, in_specs=[pl.BlockSpec(memory_space=pltpu....  56.7 us
    pallas_call x1, Pallas kernels, block_forward(): pl.pallas_call(functools.partial(block_forward_kernel, row), grid=(tables...  35.7 us
    pallas_call x1, Pallas kernels, block_backward(): pl.pallas_call(block_backward_kernel, grid=(tables,), in_specs=[per_table...  29.9 us
    pallas_call x1, Pallas kernels, widen(): pl.pallas_call(widen_kernel, in_specs=[near] + [far] * 2, out_specs=[far]...  12.7 us

commit v1 on v0

--- a/solution.py
+++ b/solution.py
@@ -15,8 +15,14 @@
 F32 = jnp.float32
 WIDE = 32
 LEAD = 40
+SLOTS = 5
+PITCH = 3
+SIZE = 1
+EARLY = (0, 2, 1, 0, 1)
+LATE = (0, 2, 1, 0, 1)
 MIB = 1024 * 1024
 MESH = pl.DeviceIdType.MESH
+LOGICAL = pl.DeviceIdType.LOGICAL
 
 
 def dot(left, right):
@@ -207,24 +213,217 @@
     )(image, weight, mean, var, scale, shift, proj, proj_bias, attn_in)
 
 
+def orders(dp, row):
+    row_digits = [("row", 1 << i, 2) for i in range(row.bit_length() - 1)]
+    far, stride = [], 2
+    while stride < dp:
+        radix = 2
+        far.append(("dp", stride, radix))
+        stride *= radix
+    pair, others, near = row_digits[:1], row_digits[1:], [("dp", 1, 2)]
+    return [pair + near + others + far, pair + others + near + far, pair + far + near + others]
+
+
+def places(dp, row, route):
+    at = {"dp": lax.axis_index("dp"), "row": lax.axis_index("row")}
+    weight = {"dp": row, "row": 1}
+    here = at["dp"] * row + at["row"]
+    peers = [lax.rem(at["row"] + d, row) for d in range(row)]
+    peer_ids = [here - at["row"] + peer for peer in peers]
+    own, partners = {}, {}
+    for digit in route:
+        axis, stride, radix = digit
+        own[digit] = [lax.rem(at[axis] // stride + d, radix) for d in range(radix)]
+        partners[digit] = [
+            here + (other - own[digit][0]) * (stride * weight[axis]) for other in own[digit]
+        ]
+    return peers, peer_ids, own, partners
+
+
+def timetable(early, late, stages, slots):
+    table, chunks, at_unit = {}, [], 0
+    for first, count, pitch, size, turns in ((0, early, PITCH, SIZE, EARLY), (slots, late, 1, 1, LATE)):
+        seen, last, i = {}, at_unit + count, 0
+        while at_unit < last:
+            stream = turns[i % len(turns)]
+            lag = seen.get(stream, 0)
+            seen[stream] = lag + 1
+            units = min(size, last - at_unit)
+            chunks.append((stream, at_unit, units))
+            at_unit, i = at_unit + units, i + 1
+            for k in range(2 * stages + 1):
+                at = first + pitch * (lag + k)
+                if pitch > 1 and at >= slots:
+                    at = slots + (at - slots) // pitch
+                table.setdefault(at, []).append((len(chunks) - 1, k))
+    return {at: steps[::-1] for at, steps in sorted(table.items())}, chunks
+
+
+class Summing:
+    def __init__(self, chunks, routes, own, partners, unit, held, landed, done, total, rows_all, sems):
+        self.chunks, self.routes, self.unit, self.partners = chunks, routes, unit, partners
+        self.held, self.landed, self.done, self.total, self.rows_all = held, landed, done, total, rows_all
+        self.send_sem, self.land_sem, self.back_sem, self.home_sem, self.out_sem = sems
+        self.stages = len(routes[0])
+        self.plans = {}
+        for stream, units in sorted({(stream, units) for stream, _, units in chunks}):
+            start, rows, slot, plan = 0, unit * units, 0, []
+            for digit in routes[stream]:
+                radix = digit[2]
+                part = rows // radix
+                targets = [start + other * part for other in own[digit]]
+                plan.append((targets, part, unit * units - rows, slot, partners[digit]))
+                start, rows, slot = targets[0], part, slot + radix - 1
+            self.plans[stream, units] = plan
+
+    def plan(self, c, s):
+        stream, _, units = self.chunks[c]
+        return self.plans[stream, units][s]
+
+    def base(self, c):
+        return self.chunks[c][1] * self.unit
+
+    def rows_at(self, c, offset, rows):
+        return pl.ds(pl.multiple_of(self.base(c) + offset, 16), rows)
+
+    def out(self, c, s):
+        targets, part, landing, slot, partners = self.plan(c, s)
+        return [
+            pltpu.make_async_remote_copy(
+                src_ref=self.held.at[self.rows_at(c, targets[d], part), :],
+                dst_ref=self.landed.at[pl.ds(self.base(c) + landing + (d - 1) * part, part), :],
+                send_sem=self.send_sem.at[c, slot + d - 1], recv_sem=self.land_sem.at[c, slot + d - 1],
+                device_id=partners[d], device_id_type=LOGICAL,
+            )
+            for d in range(1, len(partners))
+        ]
+
+    def back(self, c, s):
+        targets, part, _, slot, partners = self.plan(c, s)
+        here = self.done.at[self.rows_at(c, targets[0], part), :]
+        return [
+            pltpu.make_async_remote_copy(
+                src_ref=here, dst_ref=here,
+                send_sem=self.back_sem.at[c, slot + d - 1], recv_sem=self.home_sem.at[c, slot + d - 1],
+                device_id=partners[d], device_id_type=LOGICAL,
+            )
+            for d in range(1, len(partners))
+        ]
+
+    def collect(self, c, s, target):
+        targets, part, landing, _, partners = self.plan(c, s)
+        for copy in self.out(c, s):
+            copy.wait_recv()
+        step = min(part, 256)
+        for i in range(0, part, step):
+            here = self.rows_at(c, targets[0] + i, step)
+            found = self.held[here, :].astype(F32)
+            for d in range(len(partners) - 1):
+                found += self.landed[pl.ds(self.base(c) + landing + d * part + i, step), :].astype(F32)
+            target[here, :] = found.astype(BF)
+
+    def finish(self, c):
+        rows = pl.ds(self.base(c), min(self.unit * self.chunks[c][2], self.rows_all - self.base(c)))
+        return pltpu.make_async_copy(self.done.at[rows, :], self.total.at[rows, :], self.out_sem.at[c])
+
+    def step(self, c, k):
+        last = self.stages
+        if 0 < k < last:
+            self.collect(c, k - 1, self.held)
+        elif k == last:
+            self.collect(c, k - 1, self.done)
+        elif k > last:
+            for copy in self.back(c, 2 * last - k):
+                copy.wait_recv()
+        if k < last:
+            copies = self.out(c, k)
+        elif k < 2 * last:
+            copies = self.back(c, 2 * last - 1 - k)
+        else:
+            copies = [self.finish(c)]
+        for copy in copies:
+            copy.start()
+
+    def settle(self):
+        for c in range(len(self.chunks)):
+            for s in range(self.stages):
+                for copy in self.out(c, s) + self.back(c, s):
+                    copy.wait_send()
+            self.finish(c).wait()
+
+
 def block_backward_kernel(
+    plan, routes, unit, dp, row,
     grad_tokens, padded, hidden, block_out, slope_one, slope_two, norm_one, norm_two,
-    weight, var, scale, proj,
-    image_grad, grads, bn_sums, proj_bias_grad,
-    shifted, held, kept, weight_back, conv_sum, proj_sum, bn_sum, bias_sum,
+    weight, var, scale, proj, early, line_gain, line_bias, line_ffn_in, line_ffn_out,
+    total, small_total, image_back,
+    shifted_two, shifted_one, held, kept, weight_back, conv_sum, proj_sum, bn_sum, bias_sum, image_grad,
+    parts, landed, done, small_held, small_landed,
+    load_sem, send_sem, land_sem, back_sem, home_sem, out_sem,
+    small_send, small_land, image_send, image_land, image_sem,
 ):
     step = pl.program_id(0)
-    cells = padded.shape[1]
+    tables, cells = image_grad.shape[0], padded.shape[1]
     half = cells // 2
+    owned, rows = image_back.shape[1] // row, image_back.shape[2]
     gain = lax.rsqrt(var[...] + EPS) * scale[...]
+    peers, peer_ids, own, partners = places(dp, row, routes[0])
+    me = peers[0]
+    turns, chunks = plan
+    stages = len(routes[0])
+    early_rows = early.shape[0]
+    summing = Summing(
+        chunks, routes, own, partners, unit, parts, landed, done, total, total.shape[0],
+        (send_sem, land_sem, back_sem, home_sem, out_sem),
+    )
+    load = pltpu.make_async_copy(early, parts.at[pl.ds(0, early_rows), :], load_sem)
+
+    def image_copy(t, d):
+        return pltpu.make_async_remote_copy(
+            src_ref=image_grad.at[t, pl.ds(pl.multiple_of(peers[d] * rows, WIDE), rows)],
+            dst_ref=image_back.at[t // owned, me * owned + lax.rem(t, owned)],
+            send_sem=image_send.at[t, d - 1], recv_sem=image_land.at[t, d - 1],
+            device_id=peer_ids[d], device_id_type=LOGICAL,
+        )
+
+    def image_keep(t):
+        return pltpu.make_async_copy(
+            image_grad.at[t, pl.ds(pl.multiple_of(me * rows, WIDE), rows)],
+            image_back.at[t // owned, me * owned + lax.rem(t, owned)], image_sem.at[t],
+        )
+
+    def slot(phase):
+        for t in range(tables):
+            steps = turns.get(t * SLOTS + phase)
+            if steps:
+                @pl.when(step == t)
+                def _():
+                    for c, k in steps:
+                        summing.step(c, k)
 
     @pl.when(step == 0)
     def _():
-        clear_edges(shifted, (held,), cells)
+        load.start()
+        barrier = pltpu.get_barrier_semaphore()
+        greeted = peer_ids[1:]
+        for digit in routes[0]:
+            if digit[0] == "dp":
+                greeted = greeted + partners[digit][1:]
+        for device in greeted:
+            pl.semaphore_signal(barrier, inc=1, device_id=device, device_id_type=LOGICAL)
+        clear_edges(shifted_two, (held,), cells)
+        clear_edges(shifted_one, (), cells)
         conv_sum[...] = jnp.zeros_like(conv_sum)
         proj_sum[...] = jnp.zeros_like(proj_sum)
         bn_sum[...] = jnp.zeros_like(bn_sum)
         bias_sum[...] = jnp.zeros_like(bias_sum)
+        pl.semaphore_wait(barrier, len(greeted))
+        load.wait()
+
+    slot(0)
+
+    @pl.when(step == 0)
+    def _():
         for layer in range(2):
             for tap in range(9):
                 turned = weight[layer, tap * 256 : (tap + 1) * 256, :].T
@@ -234,7 +433,7 @@
         bn_sum[layer : layer + 1, :] += jnp.sum(grad * norm.astype(F32), axis=0, keepdims=True)
         bn_sum[2 + layer : 3 + layer, :] += jnp.sum(grad, axis=0, keepdims=True)
 
-    def add_conv(layer, inputs):
+    def add_conv(layer, inputs, shifted):
         turned = inputs.T
         for a in range(3):
             start = (2 - a) * WIDE
@@ -250,69 +449,138 @@
         kept[part, :] = grad
         add_stats(1, grad, norm_two[0, part, :])
         held[LEAD + start : LEAD + start + half, :] = grad * gain[1:2]
-    spread(shifted, held, cells)
+    slot(1)
+    spread(shifted_two, held, cells)
     for start in (0, half):
         part = slice(start, start + half)
-        back = dot(three_rows(shifted, start, half), weight_back[1])
+        back = dot(three_rows(shifted_two, start, half), weight_back[1])
         grad = slope_one[0, part, :].astype(F32) * back
         add_stats(0, grad, norm_one[0, part, :])
         held[LEAD + start : LEAD + start + half, :] = grad * gain[0:1]
-    add_conv(1, hidden[0])
-    spread(shifted, held, cells)
+    slot(2)
+    spread(shifted_one, held, cells)
     for start in (0, half):
-        back = dot(three_rows(shifted, start, half), weight_back[0]) + kept[start : start + half, :]
-        image_grad[0, start : start + half, :] = back.astype(BF)
-    add_conv(0, padded[0])
-
-    @pl.when(step == pl.num_programs(0) - 1)
+        back = dot(three_rows(shifted_one, start, half), weight_back[0]) + kept[start : start + half, :]
+        image_grad[step, start : start + half, :] = back.astype(BF)
+    for d in range(1, row):
+        image_copy(step, d).start()
+    image_keep(step).start()
+    slot(3)
+    add_conv(1, hidden[0], shifted_two)
+    slot(4)
+    add_conv(0, padded[0], shifted_one)
+
+    @pl.when(step == tables - 1)
     def _():
         for a in range(3):
             for b in range(3):
-                rows = slice((3 * a + b) * 256, (3 * a + b + 1) * 256)
+                at = early_rows + (3 * a + b) * 256
                 for layer in range(2):
-                    grads[rows, layer * 256 : (layer + 1) * 256] = conv_sum[layer, a, b].astype(BF)
-        grads[9 * 256 :, :] = proj_sum[...].astype(BF)
-        bn_sums[...] = bn_sum[...]
-        proj_bias_grad[...] = bias_sum[...]
+                    lanes = slice(layer * 256, (layer + 1) * 256)
+                    parts[at : at + 256, lanes] = conv_sum[layer, a, b].astype(BF)
+        at = early_rows + 9 * 256
+        parts[at : at + 256, :] = proj_sum[...].astype(BF)
+        small_held[0] = jnp.concatenate([
+            jnp.concatenate([bn_sum[0:2, :], bn_sum[2:4, :]], axis=1), bias_sum[...], line_ffn_out[...],
+            line_ffn_in[:, 0:512], line_ffn_in[:, 512:1024], jnp.zeros((2, 512), F32),
+            line_gain[...], line_bias[...], jnp.zeros((2, 512), F32),
+        ], axis=0)
+
+        slots = [sum(digit[2] - 1 for digit in routes[0][:s]) for s in range(stages)]
+
+        def small_copies(s):
+            return [
+                pltpu.make_async_remote_copy(
+                    src_ref=small_held.at[s], dst_ref=small_landed.at[slots[s] + d - 1],
+                    send_sem=small_send.at[slots[s] + d - 1], recv_sem=small_land.at[slots[s] + d - 1],
+                    device_id=partners[routes[0][s]][d], device_id_type=LOGICAL,
+                )
+                for d in range(1, routes[0][s][2])
+            ]
+
+        for at, steps in turns.items():
+            if at < tables * SLOTS:
+                continue
+            s = at - tables * SLOTS
+            if 0 < s <= stages:
+                found = small_held[s - 1]
+                for d, copy in enumerate(small_copies(s - 1)):
+                    copy.wait()
+                    found += small_landed[slots[s - 1] + d]
+                if s < stages:
+                    small_held[s] = found
+                else:
+                    small_total[...] = found
+            if s < stages:
+                for copy in small_copies(s):
+                    copy.start()
+            for c, k in steps:
+                summing.step(c, k)
+        summing.settle()
+        for t in range(tables):
+            for d in range(1, row):
+                image_copy(t, d).wait()
+            image_keep(t).wait()
 
 
 def block_backward(
     grad_tokens, padded, hidden, block_out, slope_one, slope_two, norm_one, norm_two,
-    weight, var, scale, proj,
+    weight, var, scale, proj, early, smalls, dp, row, batches,
 ):
     tables, cells, model = grad_tokens.shape
     width = proj.shape[0]
     per = per_table(cells, width)
-    conv_shape = (2, 3, 3, width, width)
+    once = pl.Buffered(1)
+    routes = orders(dp, row)
+    stages = len(routes[0])
+    arrivals = sum(digit[2] - 1 for digit in routes[0])
+    unit = 16 * dp * row
+    rows = early.shape[0] + 10 * width
+    early_units, units = early.shape[0] // unit, -(-rows // unit)
+    plan = timetable(early_units, units - early_units, stages, SLOTS * tables)
+    far = pl.BlockSpec(memory_space=pl.ANY)
+    near = pl.BlockSpec(memory_space=pltpu.VMEM)
+    sem = pltpu.SemaphoreType.DMA
     return pl.pallas_call(
-        block_backward_kernel,
+        functools.partial(block_backward_kernel, plan, routes, unit, dp, row),
         grid=(tables,),
         in_specs=[per_table(cells, model)] + [per] * 7
-        + [whole(*weight.shape)] + [whole(2, width)] * 2 + [whole(*proj.shape)],
-        out_specs=[
-            per, whole(10 * width, model), whole(4, width), whole(1, model),
-        ],
+        + [pl.BlockSpec(weight.shape, lambda t: (0, 0, 0), pipeline_mode=once)]
+        + [whole(2, width)] * 2 + [whole(*proj.shape)] + [far] + [whole(*x.shape) for x in smalls],
+        out_specs=[far, whole(16, model), far],
         out_shape=[
-            jax.ShapeDtypeStruct((tables, cells, width), BF),
-            jax.ShapeDtypeStruct((10 * width, model), BF),
-            jax.ShapeDtypeStruct((4, width), F32),
-            jax.ShapeDtypeStruct((1, model), F32),
+            jax.ShapeDtypeStruct((rows, model), BF),
+            jax.ShapeDtypeStruct((16, model), F32),
+            jax.ShapeDtypeStruct((batches, tables // batches * row, cells // row, width), BF),
         ],
         scratch_shapes=[
+            pltpu.VMEM((cells + 2 * WIDE, 3 * width), BF),
             pltpu.VMEM((cells + 2 * WIDE, 3 * width), BF),
             pltpu.VMEM((cells + 80, width), F32),
             pltpu.VMEM((cells, width), F32),
             pltpu.VMEM(weight.shape, BF),
-            pltpu.VMEM(conv_shape, F32),
+            pltpu.VMEM((2, 3, 3, width, width), F32),
             pltpu.VMEM(proj.shape, F32),
             pltpu.VMEM((4, width), F32),
             pltpu.VMEM((1, model), F32),
+            pltpu.VMEM((tables, cells, width), BF),
+            pltpu.VMEM((units * unit, model), BF),
+            pltpu.VMEM((units * unit, model), BF),
+            pltpu.VMEM((units * unit, model), BF),
+            pltpu.VMEM((stages, 16, model), F32),
+            pltpu.VMEM((arrivals, 16, model), F32),
+            sem, sem((units, arrivals)), sem((units, arrivals)),
+            sem((units, arrivals)), sem((units, arrivals)), sem((units,)),
+            sem((arrivals,)), sem((arrivals,)),
+            sem((tables, row - 1)), sem((tables, row - 1)), sem((tables,)),
         ],
-        compiler_params=pltpu.CompilerParams(vmem_limit_bytes=56 * MIB),
+        compiler_params=pltpu.CompilerParams(
+            vmem_limit_bytes=62 * MIB, collective_id=0, has_side_effects=True
+        ),
         name="block_backward",
     )(
         grad_tokens, padded, hidden, block_out, slope_one, slope_two, norm_one, norm_two,
-        weight, var, scale, proj,
+        weight, var, scale, proj, early, *smalls,
     )
 
 
@@ -618,236 +886,6 @@
     )
 
 
-def orders(dp, row):
-    row_bits = [("row", 1 << i) for i in range(row.bit_length() - 1)]
-    dp_bits = [("dp", 1 << i) for i in range(dp.bit_length() - 1)]
-    pair, others = row_bits[:1], row_bits[1:]
-    near, far = dp_bits[:1], dp_bits[1:]
-    return [pair + near + others + far, pair + others + near + far, pair + far + near + others]
-
-
-def plan_of(units):
-    turn = (0, 2, 1) * 4 + (0, 2, 0, 0, 0)
-    return [(turn[i % len(turn)], i, 1) for i in range(units)]
-
-
-def side_of(axis, bit):
-    return lax.rem(lax.axis_index(axis) // bit, 2)
-
-
-def partner_of(axis, bit):
-    return {axis: lax.axis_index(axis) + bit * (1 - 2 * side_of(axis, bit))}
-
-
-def add_rows(target, held, start, landed, at, rows):
-    step = 128
-    while rows % step:
-        step //= 2
-
-    def one(i, carry):
-        here = pl.ds(pl.multiple_of(start + i * step, 16), step)
-        there = pl.ds(pl.multiple_of(at + i * step, 16), step)
-        target[here, :] = held[here, :] + landed[there, :]
-        return carry
-
-    lax.fori_loop(0, rows // step, one, 0)
-
-
-def reduce_kernel(plan, streams, unit, sizes, row, *refs):
-    count = len(sizes)
-    parts, image_grad, smalls, refs = refs[:count], refs[count], refs[count + 1 : count + 7], refs[count + 7 :]
-    total, small_total, image_back = refs[:3]
-    held, landed, done, small_held, small_landed = refs[3:8]
-    load_sem, send_sem, land_sem, back_sem, home_sem = refs[8:13]
-    small_send, small_land, out_sem, image_send, image_land, image_sem = refs[13:]
-    stages = len(streams[0])
-    rows_all = sum(sizes)
-    bounds = [sum(sizes[:i]) for i in range(count + 1)]
-    loads = [
-        pltpu.make_async_copy(part, held.at[pl.ds(bounds[i], sizes[i]), :], load_sem.at[i])
-        for i, part in enumerate(parts)
-    ]
-    for copy in loads:
-        copy.start()
-    barrier = pltpu.get_barrier_semaphore()
-    me = lax.axis_index("row")
-    peers = [{"row": lax.rem(me + d, row)} for d in range(1, row)]
-    across = [partner_of(axis, bit) for axis, bit in streams[0] if axis == "dp"]
-    for device in peers + across:
-        pl.semaphore_signal(barrier, inc=1, device_id=device, device_id_type=MESH)
-    pl.semaphore_wait(barrier, len(peers) + len(across))
-    owned, rows = image_back.shape[1] // row, image_back.shape[2]
-    images = []
-    for t in range(image_grad.shape[0]):
-        target = image_back.at[t // owned, me * owned + t % owned]
-        for d in range(1, row):
-            peer = lax.rem(me + d, row)
-            images.append(pltpu.make_async_remote_copy(
-                src_ref=image_grad.at[t, pl.ds(pl.multiple_of(peer * rows, WIDE), rows)], dst_ref=target,
-                send_sem=image_send.at[t, d - 1], recv_sem=image_land.at[t, d - 1],
-                device_id={"row": peer}, device_id_type=MESH,
-            ))
-        images.append(pltpu.make_async_copy(
-            image_grad.at[t, pl.ds(pl.multiple_of(me * rows, WIDE), rows)], target, image_sem.at[t],
-        ))
-    for copy in images:
-        copy.start()
-    bn, proj_bias, gain, bias, ffn_in_bias, ffn_out_bias = smalls
-    small_held[0] = jnp.concatenate([
-        jnp.concatenate([bn[0:2, :], bn[2:4, :]], axis=1), proj_bias[...], ffn_out_bias[...],
-        ffn_in_bias[:, 0:512], ffn_in_bias[:, 512:1024], jnp.zeros((2, 512), F32),
-        gain[...], bias[...], jnp.zeros((2, 512), F32),
-    ], axis=0)
-    loaded = [False] * count
-
-    def need(first, last):
-        for i in range(count):
-            if bounds[i] < last and bounds[i + 1] > first and not loaded[i]:
-                loads[i].wait()
-                loaded[i] = True
-
-    state = [dict(start=first * unit, rows=n * unit, at=0) for _, first, n in plan]
-    flights, backs, outs = {}, {}, []
-
-    def small_step(s):
-        if s > 0:
-            flights["small", s - 1].wait()
-            both = small_held[s - 1] + small_landed[s - 1]
-            if s == stages:
-                small_total[...] = both
-                return
-            small_held[s] = both
-        axis, bit = streams[0][s]
-        copy = pltpu.make_async_remote_copy(
-            src_ref=small_held.at[s], dst_ref=small_landed.at[s],
-            send_sem=small_send.at[s], recv_sem=small_land.at[s],
-            device_id=partner_of(axis, bit), device_id_type=MESH,
-        )
-        copy.start()
-        flights["small", s] = copy
-
-    def collect(c, s, target):
-        _, first, n = plan[c]
-        now = state[c]
-        flights[c, s].wait_recv()
-        add_rows(target, held, now["start"], landed, first * unit + now["at"], now["rows"])
-        now["at"] += now["rows"]
-
-    def split(c, s):
-        stream, first, n = plan[c]
-        now = state[c]
-        axis, bit = streams[stream][s]
-        if s == 0:
-            need(first * unit, (first + n) * unit)
-        else:
-            collect(c, s - 1, held)
-        half = now["rows"] // 2
-        side = side_of(axis, bit)
-        base = now["start"]
-        copy = pltpu.make_async_remote_copy(
-            src_ref=held.at[pl.ds(pl.multiple_of(base + (1 - side) * half, 16), half), :],
-            dst_ref=landed.at[pl.ds(first * unit + now["at"], half), :],
-            send_sem=send_sem.at[c, s], recv_sem=land_sem.at[c, s],
-            device_id=partner_of(axis, bit), device_id_type=MESH,
-        )
-        copy.start()
-        flights[c, s] = copy
-        now["start"] = base + side * half
-        now["rows"] = half
-
-    def merge(c, s):
-        stream, first, n = plan[c]
-        now = state[c]
-        axis, bit = streams[stream][s]
-        if s == stages - 1:
-            collect(c, s, done)
-        else:
-            backs[c, s + 1].wait_recv()
-            now["rows"] *= 2
-            now["start"] = now["start"] - side_of(*streams[stream][s + 1]) * (now["rows"] // 2)
-        region = done.at[pl.ds(pl.multiple_of(now["start"], 16), now["rows"]), :]
-        copy = pltpu.make_async_remote_copy(
-            src_ref=region, dst_ref=region,
-            send_sem=back_sem.at[c, s], recv_sem=home_sem.at[c, s],
-            device_id=partner_of(axis, bit), device_id_type=MESH,
-        )
-        copy.start()
-        backs[c, s] = copy
-
-    def finish(c):
-        _, first, n = plan[c]
-        backs[c, 0].wait_recv()
-        last = min((first + n) * unit, rows_all)
-        if last > first * unit:
-            region = pl.ds(first * unit, last - first * unit)
-            copy = pltpu.make_async_copy(done.at[region, :], total.at[region, :], out_sem.at[c])
-            copy.start()
-            outs.append(copy)
-
-    lags, seen = [], {}
-    for stream, _, _ in plan:
-        lags.append(seen.get(stream, 0))
-        seen[stream] = lags[-1] + 1
-    for turn in range(2 * stages + 1 + max(lags)):
-        if turn <= stages:
-            small_step(turn)
-        for c, lag in reversed(list(enumerate(lags))):
-            k = turn - lag
-            if 0 <= k < stages:
-                split(c, k)
-            elif stages <= k < 2 * stages:
-                merge(c, 2 * stages - 1 - k)
-            elif k == 2 * stages:
-                finish(c)
-    for c in range(len(plan)):
-        for s in range(stages):
-            flights[c, s].wait_send()
-            backs[c, s].wait_send()
-    for copy in outs + images:
-        copy.wait()
-
-
-def reduce_all(parts, image_grad, smalls, dp, row, batches):
-    streams = orders(dp, row)
-    stages = len(streams[0])
-    sizes = [p.shape[0] for p in parts]
-    rows, width = sum(sizes), parts[0].shape[1]
-    unit = 16 * dp * row
-    plan = plan_of(-(-rows // unit))
-    chunks = len(plan)
-    tables, cells, channels = image_grad.shape
-    back = (batches, tables // batches * row, cells // row, channels)
-    small = (16, width)
-    far = pl.BlockSpec(memory_space=pl.ANY)
-    near = pl.BlockSpec(memory_space=pltpu.VMEM)
-    sem = pltpu.SemaphoreType.DMA
-    return pl.pallas_call(
-        functools.partial(reduce_kernel, plan, streams, unit, sizes, row),
-        in_specs=[far] * (len(parts) + 1) + [near] * len(smalls),
-        out_specs=[far, near, far],
-        out_shape=[
-            jax.ShapeDtypeStruct((rows, width), BF),
-            jax.ShapeDtypeStruct(small, F32),
-            jax.ShapeDtypeStruct(back, BF),
-        ],
-        scratch_shapes=[
-            pltpu.VMEM((chunks * unit, width), BF),
-            pltpu.VMEM((chunks * unit, width), BF),
-            pltpu.VMEM((chunks * unit, width), BF),
-            pltpu.VMEM((stages,) + small, F32),
-            pltpu.VMEM((stages,) + small, F32),
-            sem((len(parts),)), sem((chunks, stages)), sem((chunks, stages)),
-            sem((chunks, stages)), sem((chunks, stages)),
-            sem((stages,)), sem((stages,)), sem((chunks,)),
-            sem((tables, row - 1)), sem((tables, row - 1)), sem((tables,)),
-        ],
-        compiler_params=pltpu.CompilerParams(
-            vmem_limit_bytes=60 * MIB, collective_id=0, has_side_effects=True
-        ),
-        name="reduce_all",
-    )(*parts, image_grad, *smalls)
-
-
 def widen_kernel(
     small, total, back, conv, proj, attn_in, attn_out, ffn_in, ffn_out, image_grad,
     bn_scale, bn_shift, proj_bias, gain, bias, ffn_in_bias, ffn_out_bias,
@@ -983,14 +1021,10 @@
         memory, cross_kv, attn_in, attn_out, ln_gain, ln_bias,
         ffn_in, ffn_in_bias.reshape(1, -1), ffn_out, ffn_out_bias.reshape(1, -1),
     )
-    image_grad, block_g, bn_g, proj_bias_g = block_backward(
+    total, small, back = block_backward(
         grad_tokens, padded, hidden, block_out, slope_one, slope_two, norm_one, norm_two,
-        weight, bn_var, bn_scale, proj_weight,
-    )
-    total, small, back = reduce_all(
-        (decoder_g.reshape(-1, model), block_g), image_grad,
-        (bn_g, proj_bias_g, gain_g, bias_g, ffn_in_bias_g, ffn_out_bias_g),
-        lax.axis_size("dp"), row, batches,
+        weight, bn_var, bn_scale, proj_weight, decoder_g.reshape(-1, model),
+        (gain_g, bias_g, ffn_in_bias_g, ffn_out_bias_g), lax.axis_size("dp"), row, batches,
     )
     (
         conv_g, proj_g, attn_in_g, attn_out_g, ffn_in_g, ffn_out_g, image_g,

time: 247 us -> 218 us (0.88)
  Pallas kernels: 245 us -> 215 us
    pallas_call x2 -> x1, Pallas kernels: 140 us -> 110 us  [block_backward(): pl.pallas_call(functools.partial(block_backward_kernel, plan, routes, uni...]
where the time goes in v1:
time: 218 us
  Pallas kernels  215 us (99%)
    pallas_call x1, Pallas kernels, block_backward(): pl.pallas_call(functools.partial(block_backward_kernel, plan, routes, uni...  110 us
    pallas_call x1, Pallas kernels, decoder(): pl.pallas_call(decoder_kernel, in_specs=[pl.BlockSpec(memory_space=pltpu....  56.7 us
    pallas_call x1, Pallas kernels, block_forward(): pl.pallas_call(functools.partial(block_forward_kernel, row), grid=(tables...  35.7 us
    pallas_call x1, Pallas kernels, widen(): pl.pallas_call(widen_kernel, in_specs=[near] + [far] * 2, out_specs=[far]...  12.7 us

profile of v1, /device:TPU:1, one launch (start us, length us, event | category | flops | bytes accessed | tf_op | source)
XLA Modules:
  0.0 217.5 jit_solution(2183016433802188280)
XLA Ops:
  0.6 1.3 reshape.77.lengths
  1.9 35.7 %block_forward.1 = (bf16[4,896,256]{2,1,0:T(8,128)(2,1)}, bf16[4,896,256]{2,1,0:T(8,128)(2,1)}, bf16[4,896,256]{2,1,0:T(8,128)(2,1)}, bf16[4,896,256]{2,1,0:T(8,...) custom-call(bf16[2,1568,256]{2,1,0:T(8,128)(2,1)} %bitcast.21, ...), custom_call_target="tpu_custom_call" | custom-call | tf_op jit(solution)/shard_map/block_forward/pallas_call | solution.py:186
  37.6 56.7 %decoder.1 = (bf16[512,512]{1,0:T(8,128)(2,1)}, f32[512,512]{1,0:T(8,128)}, bf16[4,896,512]{2,1,0:T(8,128)(2,1)}, bf16[12,512,512]{2,1,0:T(8,128)(2,1)}, f32[3,5...) custom-call(s32[4]{0:T(128)} %reshape.77.lengths, f32[3,512]{1,0:T(4,128)} %ln_gain.1, ...), custom_call_target="tpu_custom_call" | custom-call | tf_op jit(solution)/shard_map/decoder/pallas_call | solution.py:845
  94.3 110.3 %block_backward.1 = (bf16[8704,512]{1,0:T(8,128)(2,1)}, f32[16,512]{1,0:T(8,128)}, bf16[2,8,224,256]{3,2,1,0:T(8,128)(2,1)}) custom-call(bf16[4,896,512]{2,1,0:T(8,128)(2,1)} %get-tuple-element.53.grad_tokens, bf16[4,896,256]{2,1,0:T(8,128)(2,1)} %get-tuple-element.54.padded, bf16[4,896,256]{2,1,0:T(8,128)(2,1)} %get-tuple-element.55.hidden, ...), custom_call_target="tpu_custom_call" | custom-call | tf_op jit(solution)/shard_map/block_backward/pallas_call | solution.py:544
  204.6 12.7 %widen.1 = (f32[2,3,3,256,256]{4,3,2,1,0:T(8,128)}, f32[256,512]{1,0:T(8,128)}, f32[6,512,512]{2,1,0:T(8,128)}, f32[2,512,512]{2,1,0:T(8,128)}, f32[512,1024]{1,...) custom-call(f32[16,512]{1,0:T(8,128)} %get-tuple-element.66.small, ...), custom_call_target="tpu_custom_call" | custom-call | tf_op jit(solution)/shard_map/widen/pallas_call | solution.py:985

commit v2 on v1

--- a/solution.py
+++ b/solution.py
@@ -70,8 +70,11 @@
 
 
 def block_forward_kernel(
-    row, image, weight, mean, var, scale, shift, proj, proj_bias, key_value,
+    row, image, lengths, tags_far, attn_in_far, attn_out_far, gain, bias,
+    weight, mean, var, scale, shift, proj, proj_bias, key_value,
     padded, hidden, block_out, slope_one, slope_two, norm_one, norm_two, memory, cross_kv,
+    qkv, self_shares, self_mix, first_in, cross_q,
+    tags, self_in, self_out, weight_sem,
     shifted, held_in, held_mid, raw, loose, sent, landed, load_sem, send_sem, land_sem, home_sem,
 ):
     table = pl.program_id(0)
@@ -109,7 +112,12 @@
     @pl.when(table == 0)
     def _():
         loads = [pltpu.make_async_copy(image.at[b], raw.at[b], load_sem.at[b]) for b in range(batches)]
-        for copy in loads:
+        fetches = [
+            pltpu.make_async_copy(tags_far, tags, weight_sem.at[0]),
+            pltpu.make_async_copy(attn_in_far.at[pl.ds(0, 4)], self_in, weight_sem.at[1]),
+            pltpu.make_async_copy(attn_out_far.at[0], self_out, weight_sem.at[2]),
+        ]
+        for copy in loads + fetches:
             copy.start()
         barrier = pltpu.get_barrier_semaphore()
         for d in range(1, row):
@@ -126,6 +134,11 @@
                     exchange(t, d).start()
                 keep(t).start()
         clear_edges(shifted, (held_in, held_mid), cells)
+        for copy in fetches:
+            copy.wait()
+        self_forward(
+            lengths, tags, self_in, self_out, gain, bias, qkv, self_shares, self_mix, first_in, cross_q
+        )
 
     for d in range(1, row):
         exchange(table, d).wait_recv()
@@ -177,23 +190,64 @@
     return pl.BlockSpec((1,) + shape, lambda t: (t,) + zeros)
 
 
-def block_forward(image, weight, mean, var, scale, shift, proj, proj_bias, attn_in, row, group, part):
+def self_forward(lengths, tags, attn_in, attn_out, gain, bias, qkv, shares, mix, first_in, cross_q):
+    tables, slots, half = shares.shape[0], shares.shape[2], 256
+    masks = lane_masks(slots, half)
+    for k in range(3):
+        qkv[k] = dot(tags[...], attn_in[k]).astype(BF)
+    key = lax.broadcasted_iota(jnp.int32, (slots, slots), 0)
+    query = lax.broadcasted_iota(jnp.int32, (slots, slots), 1)
+
+    def one(t, carry):
+        rows = pl.ds(pl.multiple_of(t * slots, slots), slots)
+        allowed = jnp.concatenate([(key <= query) & (key < lengths[t])] * GROUP, axis=1)
+        for g in range(2):
+            lanes = slice(g * half, (g + 1) * half)
+            shares[t, g], mix[rows, lanes] = attend(
+                by_head(qkv[0, rows, lanes], masks), qkv[1, rows, lanes], qkv[2, rows, lanes],
+                lambda x: jnp.where(allowed, x, MASKED),
+            )
+        return carry
+
+    lax.fori_loop(0, tables, one, 0)
+    total = tags[...].astype(F32) + dot(mix[...], attn_out[...])
+    first_in[...] = total
+    first = normalise(total)[0] * gain[0:1] + bias[0:1]
+    cross_q[...] = dot(first.astype(BF), attn_in[3]).astype(BF)
+
+
+def block_forward(
+    image, lengths, tags, attn_out, gain, bias,
+    weight, mean, var, scale, shift, proj, proj_bias, attn_in, row, group, part,
+):
     batches, width = image.shape[0], image.shape[2]
     tables, cells = batches * (group // row), part * row * WIDE
     model = proj.shape[1]
     small = jax.ShapeDtypeStruct((tables, cells, width), BF)
     stats = [whole(2, width)] * 4
+    far = pl.BlockSpec(memory_space=pl.ANY)
+    rows = tags.shape[0]
+    tag_shapes = [
+        ((3, rows, model), BF), ((tables, 2, rows // tables, GROUP * rows // tables), BF),
+        ((rows, model), BF), ((rows, model), F32), ((rows, model), BF),
+    ]
     return pl.pallas_call(
         functools.partial(block_forward_kernel, row),
         grid=(tables,),
-        in_specs=[pl.BlockSpec(memory_space=pl.ANY), whole(*weight.shape)] + stats
+        in_specs=[far, pl.BlockSpec(memory_space=pltpu.SMEM), far, far, far, whole(*gain.shape), whole(*bias.shape)]
+        + [whole(*weight.shape)] + stats
         + [whole(*proj.shape), whole(1, model), pl.BlockSpec((2,) + attn_in.shape[1:], lambda t: (2, 0, 0))],
-        out_specs=[per_table(cells, width)] * 7 + [per_table(cells, model), per_table(cells, 2 * model)],
+        out_specs=[per_table(cells, width)] * 7 + [per_table(cells, model), per_table(cells, 2 * model)]
+        + [whole(*shape) for shape, _ in tag_shapes],
         out_shape=[small] * 7 + [
             jax.ShapeDtypeStruct((tables, cells, model), BF),
             jax.ShapeDtypeStruct((tables, cells, 2 * model), BF),
-        ],
+        ] + [jax.ShapeDtypeStruct(shape, dtype) for shape, dtype in tag_shapes],
         scratch_shapes=[
+            pltpu.VMEM((rows, model), BF),
+            pltpu.VMEM((4, model, model), BF),
+            pltpu.VMEM((model, model), BF),
+            pltpu.SemaphoreType.DMA((3,)),
             pltpu.VMEM((cells + 2 * WIDE, 3 * width), BF),
             pltpu.VMEM((cells + 80, width), F32),
             pltpu.VMEM((cells + 80, width), F32),
@@ -210,7 +264,10 @@
             vmem_limit_bytes=56 * MIB, collective_id=1, has_side_effects=True
         ),
         name="block_forward",
-    )(image, weight, mean, var, scale, shift, proj, proj_bias, attn_in)
+    )(
+        image, lengths, tags, attn_in, attn_out, gain, bias,
+        weight, mean, var, scale, shift, proj, proj_bias, attn_in,
+    )
 
 
 def orders(dp, row):
@@ -594,17 +651,32 @@
     return jnp.concatenate([jnp.where(m, value, zero) for m in masks], axis=0)
 
 
-def own_lanes(stacked, masks):
-    rows = stacked.shape[0] // GROUP
-    total = stacked[0:rows]
-    for h in range(1, GROUP):
-        total = jnp.where(masks[h], stacked[h * rows : (h + 1) * rows], total)
-    return total
-
-
-def softmax_rows(scores):
-    raised = jnp.exp(scores - jnp.max(scores, axis=-1, keepdims=True))
-    return raised * (1.0 / jnp.sum(raised, axis=-1, keepdims=True))
+def own_block(turned):
+    depth, slots = turned.shape[0] // GROUP, turned.shape[1] // GROUP
+    parts = [
+        turned[h * depth : (h + 1) * depth, h * slots : (h + 1) * slots] for h in range(GROUP)
+    ]
+    return jnp.concatenate(parts, axis=0).T
+
+
+def softmax_keys(scores):
+    raised = jnp.exp(scores - jnp.max(scores, axis=0, keepdims=True))
+    return raised * (1.0 / jnp.sum(raised, axis=0, keepdims=True))
+
+
+def attend(query, key, value, hidden):
+    shares = softmax_keys(hidden(dot_nt(key, query) * 0.125)).astype(BF)
+    return shares, own_block(dot_tn(value, shares)).astype(BF)
+
+
+def attend_back(query, key, value, low, upstream):
+    shares = low.astype(F32)
+    grad_shares = dot_nt(value, upstream)
+    mean = jnp.sum(grad_shares * shares, axis=0, keepdims=True)
+    grad_scores = (shares * (grad_shares - mean)).astype(BF)
+    grad_query = (own_block(dot_tn(key, grad_scores)) * 0.125).astype(BF)
+    grad_key = (dot(grad_scores, query) * 0.125).astype(BF)
+    return grad_query, grad_key, dot(low, upstream).astype(BF)
 
 
 def normalise(value):
@@ -625,12 +697,12 @@
 
 
 def decoder_kernel(
-    lengths, ln_gain, ln_bias, ffn_in_bias, ffn_out_bias,
-    tags_far, cotangent_far, memory_far, cross_kv_far, attn_in_far, attn_out_far, ffn_in_far, ffn_out_far,
+    ln_gain, ln_bias, ffn_in_bias, ffn_out_bias,
+    qkv_far, shares_far, mix_far, first_far, cross_q_far, tags_far, cotangent_far, memory_far, cross_kv_far, attn_in_far, attn_out_far, ffn_in_far, ffn_out_far,
     decoded, tags_grad, grad_tokens, grads_far,
     ln_gain_grad, ln_bias_grad, ffn_in_bias_grad, ffn_out_bias_grad,
     tags, cotangent, memory, cross_kv, attn_in, attn_out, ffn_in, ffn_out,
-    qkv, mix, self_shares, cross_shares, cross_q, up, grad_qkv, grad_q, grad_kv, pair_sum,
+    qkv, mix, self_shares, first_in, cross_shares, cross_q, up, grad_qkv, grad_q, grad_kv, pair_sum,
     staged, weight_sem, kv_sem, memory_sem, staged_sem,
     grads, grad_sem,
 ):
@@ -651,29 +723,22 @@
     fetches = [
         pltpu.make_async_copy(far, near, weight_sem.at[i])
         for i, (far, near) in enumerate(
-            [(tags_far, tags)]
-            + [(attn_in_far.at[k], attn_in.at[k]) for k in range(4)]
-            + [(attn_out_far, attn_out), (cotangent_far, cotangent)]
-            + [(ffn_in_far, ffn_in), (ffn_out_far, ffn_out)]
-            + [(attn_in_far.at[k], attn_in.at[k]) for k in (4, 5)]
+            [(first_far, first_in), (cross_q_far, cross_q), (attn_out_far, attn_out)]
+            + [(cotangent_far, cotangent), (ffn_in_far, ffn_in), (ffn_out_far, ffn_out)]
+            + [(attn_in_far, attn_in), (qkv_far, qkv), (shares_far, self_shares)]
+            + [(mix_far, mix.at[0]), (tags_far, tags)]
         )
     ]
-    for copy in fetches[:6]:
+    for copy in fetches[:2]:
         copy.start()
     for t in range(tables):
         fetch_kv(t).start()
-    for copy in fetches[6:]:
+    for copy in fetches[2:]:
         copy.start()
     fetch_memory(0).start()
     half = 256
     wide_f32 = lane_masks(slots, half)
-    real_key = lax.rem(lax.broadcasted_iota(jnp.int32, (GROUP * slots, cells), 1), WIDE) < 28
-
-    def allowed_of(t):
-        row = lax.broadcasted_iota(jnp.int32, (slots, slots), 0)
-        col = lax.broadcasted_iota(jnp.int32, (slots, slots), 1)
-        once = (col <= row) & (col < lengths[t])
-        return jnp.concatenate([once] * GROUP, axis=0)
+    real_key = real_columns(cells)
 
     def put_grad(i, value):
         grads[i] = value.astype(BF)
@@ -682,30 +747,11 @@
         puts.append(copy)
 
     puts = []
-    fetches[0].wait()
-    for k in range(3):
-        fetches[1 + k].wait()
-        qkv[k] = dot(tags[...], attn_in[k]).astype(BF)
-
-    def self_forward(t, carry):
-        rows = pl.ds(pl.multiple_of(t * slots, slots), slots)
-        allowed = allowed_of(t)
-        for g in range(2):
-            lanes = slice(g * half, (g + 1) * half)
-            query = by_head(qkv[0, rows, lanes], wide_f32)
-            scores = dot_nt(query, qkv[1, rows, lanes]) * 0.125
-            shares = softmax_rows(jnp.where(allowed, scores, MASKED)).astype(BF)
-            self_shares[t, g] = shares
-            mix[0, rows, lanes] = own_lanes(dot(shares, qkv[2, rows, lanes]), wide_f32).astype(BF)
-        return carry
-
-    lax.fori_loop(0, tables, self_forward, 0)
-    fetches[5].wait()
-    first_unit, first_inv = normalise(tags[...].astype(F32) + dot(mix[0], attn_out[0]))
+    for copy in fetches[:2]:
+        copy.wait()
+    first_unit, first_inv = normalise(first_in[...])
     first = first_unit * ln_gain[0:1] + ln_bias[0:1]
     first_low = first.astype(BF)
-    fetches[4].wait()
-    cross_q[...] = dot(first_low, attn_in[3]).astype(BF)
 
     def cross_forward(t, carry):
         fetch_kv(t).wait()
@@ -713,18 +759,18 @@
         for g in range(2):
             lanes = slice(g * half, (g + 1) * half)
             query = by_head(cross_q[rows, lanes], wide_f32)
-            scores = dot_nt(query, cross_kv[t, :, lanes]) * 0.125
-            shares = softmax_rows(jnp.where(real_key, scores, MASKED)).astype(BF)
-            cross_shares[t, g] = shares
             value = cross_kv[t, :, 512 + g * half : 512 + (g + 1) * half]
-            mix[1, rows, lanes] = own_lanes(dot(shares, value), wide_f32).astype(BF)
+            cross_shares[t, g], mix[1, rows, lanes] = attend(
+                query, cross_kv[t, :, lanes], value, lambda x: jnp.where(real_key, x, MASKED)
+            )
         return carry
 
     lax.fori_loop(0, tables, cross_forward, 0)
+    fetches[2].wait()
     second_unit, second_inv = normalise(first + dot(mix[1], attn_out[1]))
     second = second_unit * ln_gain[1:2] + ln_bias[1:2]
     second_low = second.astype(BF)
-    for copy in fetches[6:]:
+    for copy in fetches[3:6]:
         copy.wait()
     act, slope = gelu_pair(dot(second_low, ffn_in[...]) + ffn_in_bias[...])
     inner_act = act.astype(BF)
@@ -753,6 +799,8 @@
     put_grad(7, dot_tn(mix[1], grad_cross_out))
     up[...] = dot_nt(grad_cross_out, attn_out[1]).astype(BF)
     pair_sum[...] = jnp.zeros_like(pair_sum)
+    for copy in fetches[6:]:
+        copy.wait()
 
     def cross_back(t, carry):
         @pl.when(t + 1 < tables)
@@ -765,16 +813,9 @@
             value_lanes = slice(512 + g * half, 512 + (g + 1) * half)
             query = by_head(cross_q[rows, lanes], wide_f32)
             upstream = by_head(up[rows, lanes], wide_f32)
-            low = cross_shares[t, g]
-            shares = low.astype(F32)
-            grad_shares = dot_nt(upstream, cross_kv[t, :, value_lanes])
-            mean = jnp.sum(grad_shares * shares, axis=-1, keepdims=True)
-            grad_scores = (shares * (grad_shares - mean)).astype(BF)
-            grad_q[rows, lanes] = (
-                own_lanes(dot(grad_scores, cross_kv[t, :, lanes]), wide_f32) * 0.125
-            ).astype(BF)
-            grad_kv[:, lanes] = (dot_tn(grad_scores, query) * 0.125).astype(BF)
-            grad_kv[:, value_lanes] = dot_tn(low, upstream).astype(BF)
+            grad_q[rows, lanes], grad_kv[:, lanes], grad_kv[:, value_lanes] = attend_back(
+                query, cross_kv[t, :, lanes], cross_kv[t, :, value_lanes], cross_shares[t, g], upstream
+            )
         @pl.when(t >= 2)
         def _():
             put_tokens(t - 2).wait()
@@ -808,16 +849,9 @@
             lanes = slice(g * half, (g + 1) * half)
             query = by_head(qkv[0, rows, lanes], wide_f32)
             upstream = by_head(up[rows, lanes], wide_f32)
-            low = self_shares[t, g]
-            shares = low.astype(F32)
-            grad_shares = dot_nt(upstream, qkv[2, rows, lanes])
-            mean = jnp.sum(grad_shares * shares, axis=-1, keepdims=True)
-            grad_scores = (shares * (grad_shares - mean)).astype(BF)
-            grad_qkv[0, rows, lanes] = (
-                own_lanes(dot(grad_scores, qkv[1, rows, lanes]), wide_f32) * 0.125
-            ).astype(BF)
-            grad_qkv[1, rows, lanes] = (dot_tn(grad_scores, query) * 0.125).astype(BF)
-            grad_qkv[2, rows, lanes] = dot_tn(low, upstream).astype(BF)
+            grad_qkv[0, rows, lanes], grad_qkv[1, rows, lanes], grad_qkv[2, rows, lanes] = attend_back(
+                query, qkv[1, rows, lanes], qkv[2, rows, lanes], self_shares[t, g], upstream
+            )
         return carry
 
     lax.fori_loop(0, tables, self_back, 0)
@@ -831,7 +865,7 @@
 
 
 def decoder(
-    lengths, tags, cotangent, memory, cross_kv, attn_in, attn_out, ln_gain, ln_bias,
+    kept, tags, cotangent, memory, cross_kv, attn_in, attn_out, ln_gain, ln_bias,
     ffn_in, ffn_in_bias, ffn_out, ffn_out_bias,
 ):
     tables, cells, model = memory.shape
@@ -844,7 +878,7 @@
     stacked = GROUP * slots
     return pl.pallas_call(
         decoder_kernel,
-        in_specs=[pl.BlockSpec(memory_space=pltpu.SMEM)] + [here] * 4 + [far] * 8,
+        in_specs=[here] * 4 + [far] * 13,
         out_specs=[here] * 2 + [far] * 2 + [here] * 4,
         out_shape=[
             shape((rows, model), BF), shape((rows, model), F32), shape((tables, cells, model), BF),
@@ -862,8 +896,9 @@
             pltpu.VMEM(ffn_out.shape, BF),
             pltpu.VMEM((3, rows, model), BF),
             pltpu.VMEM((2, rows, model), BF),
-            pltpu.VMEM((tables, 2, stacked, slots), BF),
-            pltpu.VMEM((tables, 2, stacked, cells), BF),
+            pltpu.VMEM((tables, 2, slots, stacked), BF),
+            pltpu.VMEM((rows, model), F32),
+            pltpu.VMEM((tables, 2, cells, stacked), BF),
             pltpu.VMEM((rows, model), BF),
             pltpu.VMEM((rows, model), BF),
             pltpu.VMEM((3, rows, model), BF),
@@ -881,7 +916,7 @@
         compiler_params=pltpu.CompilerParams(vmem_limit_bytes=60 * MIB),
         name="decoder",
     )(
-        lengths, ln_gain, ln_bias, ffn_in_bias, ffn_out_bias,
+        ln_gain, ln_bias, ffn_in_bias, ffn_out_bias, *kept,
         tags, cotangent, memory, cross_kv, attn_in, attn_out, ffn_in, ffn_out,
     )
 
@@ -1012,12 +1047,13 @@
     flat_image = image.transpose(0, 2, 3, 1, 4).reshape(batches, part * breadth * group, width)
     weight = conv_weight.reshape(2, 9 * width, width)
     forward = block_forward(
-        flat_image, weight, bn_mean, bn_var, bn_scale, bn_shift,
+        flat_image, tag_lengths.reshape(-1), tags.reshape(-1, model), attn_out, ln_gain, ln_bias,
+        weight, bn_mean, bn_var, bn_scale, bn_shift,
         proj_weight, proj_bias.reshape(1, -1), attn_in, row, group, part,
     )
-    padded, hidden, block_out, slope_one, slope_two, norm_one, norm_two, memory, cross_kv = forward
+    padded, hidden, block_out, slope_one, slope_two, norm_one, norm_two, memory, cross_kv = forward[:9]
     decoded, tags_grad, grad_tokens, decoder_g, gain_g, bias_g, ffn_in_bias_g, ffn_out_bias_g = decoder(
-        tag_lengths.reshape(-1), tags.reshape(-1, model), cotangent.reshape(-1, model),
+        forward[9:], tags.reshape(-1, model), cotangent.reshape(-1, model),
         memory, cross_kv, attn_in, attn_out, ln_gain, ln_bias,
         ffn_in, ffn_in_bias.reshape(1, -1), ffn_out, ffn_out_bias.reshape(1, -1),
     )

time: 218 us -> 214 us (0.982)
  Pallas kernels: 215 us -> 212 us
    pallas_call x1, Pallas kernels: 56.7 us -> 51.1 us  [decoder(): pl.pallas_call(decoder_kernel, in_specs=[here] * 4 + [far] * 13, out_spec...]
where the time goes in v2:
time: 214 us
  Pallas kernels  212 us (99%)
    pallas_call x1, Pallas kernels, block_backward(): pl.pallas_call(functools.partial(block_backward_kernel, plan, routes, uni...  110 us
    pallas_call x1, Pallas kernels, decoder(): pl.pallas_call(decoder_kernel, in_specs=[here] * 4 + [far] * 13, out_spec...  51.1 us
    pallas_call x1, Pallas kernels, block_forward(): pl.pallas_call(functools.partial(block_forward_kernel, row), grid=(tables...  37.5 us
    pallas_call x1, Pallas kernels, widen(): pl.pallas_call(widen_kernel, in_specs=[near] + [far] * 2, out_specs=[far]...  12.7 us

profile of v2, /device:TPU:1, one launch (start us, length us, event | category | flops | bytes accessed | tf_op | source)
XLA Modules:
  0.0 213.8 jit_solution(608812107535207696)
XLA Ops:
  0.6 1.3 reshape.81.lengths
  1.9 37.5 %block_forward.1 = (bf16[4,896,256]{2,1,0:T(8,128)(2,1)}, bf16[4,896,256]{2,1,0:T(8,128)(2,1)}, bf16[4,896,256]{2,1,0:T(8,128)(2,1)}, bf16[4,896,256]{2,1,0:T(8,...) custom-call(bf16[2,1568,256]{2,1,0:T(8,128)(2,1)} %bitcast.23, ...), custom_call_target="tpu_custom_call" | custom-call | tf_op jit(solution)/shard_map/block_forward/pallas_call | solution.py:234
  39.5 51.1 %decoder.1 = (bf16[512,512]{1,0:T(8,128)(2,1)}, f32[512,512]{1,0:T(8,128)}, bf16[4,896,512]{2,1,0:T(8,128)(2,1)}, bf16[12,512,512]{2,1,0:T(8,128)(2,1)}, f32[3,5...) custom-call(f32[3,512]{1,0:T(4,128)} %ln_gain.1, f32[3,512]{1,0:T(4,128)} %ln_bias.1, ...), custom_call_target="tpu_custom_call" | custom-call | tf_op jit(solution)/shard_map/decoder/pallas_call | solution.py:879
  90.6 110.3 %block_backward.1 = (bf16[8704,512]{1,0:T(8,128)(2,1)}, f32[16,512]{1,0:T(8,128)}, bf16[2,8,224,256]{3,2,1,0:T(8,128)(2,1)}) custom-call(bf16[4,896,512]{2,1,0:T(8,128)(2,1)} %get-tuple-element.63.grad_tokens, bf16[4,896,256]{2,1,0:T(8,128)(2,1)} %get-tuple-element.64.padded, bf16[4,896,256]{2,1,0:T(8,128)(2,1)} %get-tuple-element.65.hidden, ...), custom_call_target="tpu_custom_call" | custom-call | tf_op jit(solution)/shard_map/block_backward/pallas_call | solution.py:601
  200.8 12.7 %widen.1 = (f32[2,3,3,256,256]{4,3,2,1,0:T(8,128)}, f32[256,512]{1,0:T(8,128)}, f32[6,512,512]{2,1,0:T(8,128)}, f32[2,512,512]{2,1,0:T(8,128)}, f32[512,1024]{1,...) custom-call(f32[16,512]{1,0:T(8,128)} %get-tuple-element.76.small, ...), custom_call_target="tpu_custom_call" | custom-call | tf_op jit(solution)/shard_map/widen/pallas_call | solution.py:1020

commit v3 on v2

--- a/solution.py
+++ b/solution.py
@@ -71,10 +71,10 @@
 
 def block_forward_kernel(
     row, image, lengths, tags_far, attn_in_far, attn_out_far, gain, bias,
-    weight, mean, var, scale, shift, proj, proj_bias, key_value,
+    weight_far, mean, var, scale, shift, proj, proj_bias,
     padded, hidden, block_out, slope_one, slope_two, norm_one, norm_two, memory, cross_kv,
     qkv, self_shares, self_mix, first_in, cross_q,
-    tags, self_in, self_out, weight_sem,
+    tags, self_in, self_out, weight, key_value, weight_sem,
     shifted, held_in, held_mid, raw, loose, sent, landed, load_sem, send_sem, land_sem, home_sem,
 ):
     table = pl.program_id(0)
@@ -102,7 +102,7 @@
         gap = jnp.zeros((WIDE - 28, 128), F32)
         for h in range(2):
             lanes = slice(h * 128, (h + 1) * 128)
-            loose[h] = raw[b, :, lanes].astype(F32)
+            loose[h, 0 : raw.shape[1]] = raw[b, :, lanes].astype(F32)
             for g in range(group):
                 for r in range(rows // WIDE):
                     line = loose[h, pl.ds(r * 28 * group + g, 28, stride=group), :]
@@ -116,6 +116,8 @@
             pltpu.make_async_copy(tags_far, tags, weight_sem.at[0]),
             pltpu.make_async_copy(attn_in_far.at[pl.ds(0, 4)], self_in, weight_sem.at[1]),
             pltpu.make_async_copy(attn_out_far.at[0], self_out, weight_sem.at[2]),
+            pltpu.make_async_copy(weight_far, weight, weight_sem.at[3]),
+            pltpu.make_async_copy(attn_in_far.at[pl.ds(4, 2)], key_value, weight_sem.at[4]),
         ]
         for copy in loads + fetches:
             copy.start()
@@ -191,7 +193,7 @@
 
 
 def self_forward(lengths, tags, attn_in, attn_out, gain, bias, qkv, shares, mix, first_in, cross_q):
-    tables, slots, half = shares.shape[0], shares.shape[2], 256
+    tables, slots, half, owned = shares.shape[0], shares.shape[2], 256, lengths.shape[1]
     masks = lane_masks(slots, half)
     for k in range(3):
         qkv[k] = dot(tags[...], attn_in[k]).astype(BF)
@@ -200,7 +202,8 @@
 
     def one(t, carry):
         rows = pl.ds(pl.multiple_of(t * slots, slots), slots)
-        allowed = jnp.concatenate([(key <= query) & (key < lengths[t])] * GROUP, axis=1)
+        length = lengths[t // owned, lax.rem(t, owned)]
+        allowed = jnp.concatenate([(key <= query) & (key < length)] * GROUP, axis=1)
         for g in range(2):
             lanes = slice(g * half, (g + 1) * half)
             shares[t, g], mix[rows, lanes] = attend(
@@ -235,8 +238,8 @@
         functools.partial(block_forward_kernel, row),
         grid=(tables,),
         in_specs=[far, pl.BlockSpec(memory_space=pltpu.SMEM), far, far, far, whole(*gain.shape), whole(*bias.shape)]
-        + [whole(*weight.shape)] + stats
-        + [whole(*proj.shape), whole(1, model), pl.BlockSpec((2,) + attn_in.shape[1:], lambda t: (2, 0, 0))],
+        + [far] + stats
+        + [whole(*proj.shape), whole(1, model)],
         out_specs=[per_table(cells, width)] * 7 + [per_table(cells, model), per_table(cells, 2 * model)]
         + [whole(*shape) for shape, _ in tag_shapes],
         out_shape=[small] * 7 + [
@@ -247,12 +250,14 @@
             pltpu.VMEM((rows, model), BF),
             pltpu.VMEM((4, model, model), BF),
             pltpu.VMEM((model, model), BF),
-            pltpu.SemaphoreType.DMA((3,)),
+            pltpu.VMEM(weight.shape, BF),
+            pltpu.VMEM((2, model, model), BF),
+            pltpu.SemaphoreType.DMA((5,)),
             pltpu.VMEM((cells + 2 * WIDE, 3 * width), BF),
             pltpu.VMEM((cells + 80, width), F32),
             pltpu.VMEM((cells + 80, width), F32),
             pltpu.VMEM(image.shape, BF),
-            pltpu.VMEM((2, image.shape[1], 128), F32),
+            pltpu.VMEM((2, image.shape[1] + 8 * group, 128), F32),
             pltpu.VMEM((tables, row, part * WIDE, width), BF),
             pltpu.VMEM((tables, cells, width), BF),
             pltpu.SemaphoreType.DMA((batches,)),
@@ -266,7 +271,7 @@
         name="block_forward",
     )(
         image, lengths, tags, attn_in, attn_out, gain, bias,
-        weight, mean, var, scale, shift, proj, proj_bias, attn_in,
+        weight, mean, var, scale, shift, proj, proj_bias,
     )
 
 
@@ -412,11 +417,11 @@
 def block_backward_kernel(
     plan, routes, unit, dp, row,
     grad_tokens, padded, hidden, block_out, slope_one, slope_two, norm_one, norm_two,
-    weight, var, scale, proj, early, line_gain, line_bias, line_ffn_in, line_ffn_out,
+    weight_far, var, scale, proj, early, line_gain, line_bias, line_ffn_in, line_ffn_out,
     total, small_total, image_back,
-    shifted_two, shifted_one, held, kept, weight_back, conv_sum, proj_sum, bn_sum, bias_sum, image_grad,
+    shifted_two, shifted_one, held, kept, weight, weight_back, conv_sum, proj_sum, bn_sum, bias_sum, image_grad,
     parts, landed, done, small_held, small_landed,
-    load_sem, send_sem, land_sem, back_sem, home_sem, out_sem,
+    load_sem, turn_sem, send_sem, land_sem, back_sem, home_sem, out_sem,
     small_send, small_land, image_send, image_land, image_sem,
 ):
     step = pl.program_id(0)
@@ -433,7 +438,18 @@
         chunks, routes, own, partners, unit, parts, landed, done, total, total.shape[0],
         (send_sem, land_sem, back_sem, home_sem, out_sem),
     )
-    load = pltpu.make_async_copy(early, parts.at[pl.ds(0, early_rows), :], load_sem)
+    early_units = early_rows // unit
+
+    def load(c):
+        here = pl.ds(c * unit, unit)
+        return pltpu.make_async_copy(early.at[here, :], parts.at[here, :], load_sem.at[c])
+
+    def advance(c, k):
+        if k == 0 and c < early_units:
+            load(c).wait()
+        summing.step(c, k)
+
+    turn = pltpu.make_async_copy(weight_far, weight, turn_sem)
 
     def image_copy(t, d):
         return pltpu.make_async_remote_copy(
@@ -456,11 +472,13 @@
                 @pl.when(step == t)
                 def _():
                     for c, k in steps:
-                        summing.step(c, k)
+                        advance(c, k)
 
     @pl.when(step == 0)
     def _():
-        load.start()
+        for c in range(early_units):
+            load(c).start()
+        turn.start()
         barrier = pltpu.get_barrier_semaphore()
         greeted = peer_ids[1:]
         for digit in routes[0]:
@@ -475,12 +493,12 @@
         bn_sum[...] = jnp.zeros_like(bn_sum)
         bias_sum[...] = jnp.zeros_like(bias_sum)
         pl.semaphore_wait(barrier, len(greeted))
-        load.wait()
 
     slot(0)
 
     @pl.when(step == 0)
     def _():
+        turn.wait()
         for layer in range(2):
             for tap in range(9):
                 turned = weight[layer, tap * 256 : (tap + 1) * 256, :].T
@@ -572,7 +590,7 @@
                 for copy in small_copies(s):
                     copy.start()
             for c, k in steps:
-                summing.step(c, k)
+                advance(c, k)
         summing.settle()
         for t in range(tables):
             for d in range(1, row):
@@ -587,7 +605,6 @@
     tables, cells, model = grad_tokens.shape
     width = proj.shape[0]
     per = per_table(cells, width)
-    once = pl.Buffered(1)
     routes = orders(dp, row)
     stages = len(routes[0])
     arrivals = sum(digit[2] - 1 for digit in routes[0])
@@ -602,8 +619,7 @@
         functools.partial(block_backward_kernel, plan, routes, unit, dp, row),
         grid=(tables,),
         in_specs=[per_table(cells, model)] + [per] * 7
-        + [pl.BlockSpec(weight.shape, lambda t: (0, 0, 0), pipeline_mode=once)]
-        + [whole(2, width)] * 2 + [whole(*proj.shape)] + [far] + [whole(*x.shape) for x in smalls],
+        + [far] + [whole(2, width)] * 2 + [whole(*proj.shape)] + [far] + [whole(*x.shape) for x in smalls],
         out_specs=[far, whole(16, model), far],
         out_shape=[
             jax.ShapeDtypeStruct((rows, model), BF),
@@ -616,6 +632,7 @@
             pltpu.VMEM((cells + 80, width), F32),
             pltpu.VMEM((cells, width), F32),
             pltpu.VMEM(weight.shape, BF),
+            pltpu.VMEM(weight.shape, BF),
             pltpu.VMEM((2, 3, 3, width, width), F32),
             pltpu.VMEM(proj.shape, F32),
             pltpu.VMEM((4, width), F32),
@@ -626,7 +643,7 @@
             pltpu.VMEM((units * unit, model), BF),
             pltpu.VMEM((stages, 16, model), F32),
             pltpu.VMEM((arrivals, 16, model), F32),
-            sem, sem((units, arrivals)), sem((units, arrivals)),
+            sem((early_units,)), sem, sem((units, arrivals)), sem((units, arrivals)),
             sem((units, arrivals)), sem((units, arrivals)), sem((units,)),
             sem((arrivals,)), sem((arrivals,)),
             sem((tables, row - 1)), sem((tables, row - 1)), sem((tables,)),
@@ -997,7 +1014,8 @@
                     wide_image[b, h, pl.ds(r * 28 * group + g, 28, stride=group), :] = line[0:28, lanes]
         for h in range(2):
             waits.append(pltpu.make_async_copy(
-                wide_image.at[b, h], image_grad.at[b, :, pl.ds(h * 128, 128)], image_out.at[b, h]
+                wide_image.at[b, h, pl.ds(0, image_grad.shape[1])],
+                image_grad.at[b, :, pl.ds(h * 128, 128)], image_out.at[b, h],
             ))
             waits[-1].start()
     for copies in pending[-slots:] + [waits]:
@@ -1026,7 +1044,7 @@
             pltpu.VMEM((rows, model), BF),
             pltpu.VMEM((4, 512, model), F32),
             pltpu.VMEM((batches * group,) + back.shape[2:], BF),
-            pltpu.VMEM((batches, 2, image_shape[1], 128), F32),
+            pltpu.VMEM((batches, 2, image_shape[1] + 8 * group, 128), F32),
             sem((units,)), sem((4, 4)), sem((batches * group,)), sem((batches, 2)),
         ],
         compiler_params=pltpu.CompilerParams(vmem_limit_bytes=60 * MIB),
@@ -1047,7 +1065,7 @@
     flat_image = image.transpose(0, 2, 3, 1, 4).reshape(batches, part * breadth * group, width)
     weight = conv_weight.reshape(2, 9 * width, width)
     forward = block_forward(
-        flat_image, tag_lengths.reshape(-1), tags.reshape(-1, model), attn_out, ln_gain, ln_bias,
+        flat_image, tag_lengths, tags.reshape(-1, model), attn_out, ln_gain, ln_bias,
         weight, bn_mean, bn_var, bn_scale, bn_shift,
         proj_weight, proj_bias.reshape(1, -1), attn_in, row, group, part,
     )

time: 214 us -> 213 us (level)
  no operation moved by 1% of the time
where the time goes in v3:
time: 213 us; the launch traced here: 212 us
  Pallas kernels  211 us (99%)
    pallas_call x1, Pallas kernels, block_backward(): pl.pallas_call(functools.partial(block_backward_kernel, plan, routes, uni...  110 us
    pallas_call x1, Pallas kernels, decoder(): pl.pallas_call(decoder_kernel, in_specs=[here] * 4 + [far] * 13, out_spec...  51.1 us
    pallas_call x1, Pallas kernels, block_forward(): pl.pallas_call(functools.partial(block_forward_kernel, row), grid=(tables...  37.4 us
    pallas_call x1, Pallas kernels, widen(): pl.pallas_call(widen_kernel, in_specs=[near] + [far] * 2, out_specs=[far]...  12.7 us

profile of v3, /device:TPU:1, one launch (start us, length us, event | category | flops | bytes accessed | tf_op | source)
XLA Modules:
  0.0 212.3 jit_solution(15286628634529638118)
XLA Ops:
  0.6 37.4 %block_forward.1 = (bf16[4,896,256]{2,1,0:T(8,128)(2,1)}, bf16[4,896,256]{2,1,0:T(8,128)(2,1)}, bf16[4,896,256]{2,1,0:T(8,128)(2,1)}, bf16[4,896,256]{2,1,0:T(8,...) custom-call(bf16[2,1568,256]{2,1,0:T(8,128)(2,1)} %bitcast.23, ...), custom_call_target="tpu_custom_call" | custom-call | tf_op jit(solution)/shard_map/block_forward/pallas_call | solution.py:237
  38.0 51.1 %decoder.1 = (bf16[512,512]{1,0:T(8,128)(2,1)}, f32[512,512]{1,0:T(8,128)}, bf16[4,896,512]{2,1,0:T(8,128)(2,1)}, bf16[12,512,512]{2,1,0:T(8,128)(2,1)}, f32[3,5...) custom-call(f32[3,512]{1,0:T(4,128)} %ln_gain.1, f32[3,512]{1,0:T(4,128)} %ln_bias.1, ...), custom_call_target="tpu_custom_call" | custom-call | tf_op jit(solution)/shard_map/decoder/pallas_call | solution.py:896
  89.1 110.2 %block_backward.1 = (bf16[8704,512]{1,0:T(8,128)(2,1)}, f32[16,512]{1,0:T(8,128)}, bf16[2,8,224,256]{3,2,1,0:T(8,128)(2,1)}) custom-call(bf16[4,896,512]{2,1,0:T(8,128)(2,1)} %get-tuple-element.63.grad_tokens, bf16[4,896,256]{2,1,0:T(8,128)(2,1)} %get-tuple-element.64.padded, bf16[4,896,256]{2,1,0:T(8,128)(2,1)} %get-tuple-element.65.hidden, ...), custom_call_target="tpu_custom_call" | custom-call | tf_op jit(solution)/shard_map/block_backward/pallas_call | solution.py:618
  199.4 12.7 %widen.1 = (f32[2,3,3,256,256]{4,3,2,1,0:T(8,128)}, f32[256,512]{1,0:T(8,128)}, f32[6,512,512]{2,1,0:T(8,128)}, f32[2,512,512]{2,1,0:T(8,128)}, f32[512,1024]{1,...) custom-call(f32[16,512]{1,0:T(8,128)} %get-tuple-element.76.small, ...), custom_call_target="tpu_custom_call" | custom-call | tf_op jit(solution)/shard_map/widen/pallas_call | solution.py:1038

commit v4 on v3

--- a/solution.py
+++ b/solution.py
@@ -318,7 +318,7 @@
                 if pitch > 1 and at >= slots:
                     at = slots + (at - slots) // pitch
                 table.setdefault(at, []).append((len(chunks) - 1, k))
-    return {at: steps[::-1] for at, steps in sorted(table.items())}, chunks
+    return {at: sorted(steps, key=lambda step: step[1]) for at, steps in sorted(table.items())}, chunks
 
 
 class Summing:
@@ -682,7 +682,7 @@
 
 
 def attend(query, key, value, hidden):
-    shares = softmax_keys(hidden(dot_nt(key, query) * 0.125)).astype(BF)
+    shares = softmax_keys(hidden(dot_nt(key, query * 0.125))).astype(BF)
     return shares, own_block(dot_tn(value, shares)).astype(BF)
 
 
@@ -692,7 +692,7 @@
     mean = jnp.sum(grad_shares * shares, axis=0, keepdims=True)
     grad_scores = (shares * (grad_shares - mean)).astype(BF)
     grad_query = (own_block(dot_tn(key, grad_scores)) * 0.125).astype(BF)
-    grad_key = (dot(grad_scores, query) * 0.125).astype(BF)
+    grad_key = dot(grad_scores, query * 0.125).astype(BF)
     return grad_query, grad_key, dot(low, upstream).astype(BF)
 
 

time: 213 us -> 212 us (level)
  no operation moved by 1% of the time
where the time goes in v4:
time: 212 us; the launch traced here: 211 us
  Pallas kernels  211 us (100%)
    pallas_call x1, Pallas kernels, block_backward(): pl.pallas_call(functools.partial(block_backward_kernel, plan, routes, uni...  110 us
    pallas_call x1, Pallas kernels, decoder(): pl.pallas_call(decoder_kernel, in_specs=[here] * 4 + [far] * 13, out_spec...  50.9 us
    pallas_call x1, Pallas kernels, block_forward(): pl.pallas_call(functools.partial(block_forward_kernel, row), grid=(tables...  37.4 us
    pallas_call x1, Pallas kernels, widen(): pl.pallas_call(widen_kernel, in_specs=[near] + [far] * 2, out_specs=[far]...  12.7 us

profile of v4, /device:TPU:1, one launch (start us, length us, event | category | flops | bytes accessed | tf_op | source)
XLA Modules:
  0.0 211.5 jit_solution(2553495679040419713)
XLA Ops:
  0.6 37.4 %block_forward.1 = (bf16[4,896,256]{2,1,0:T(8,128)(2,1)}, bf16[4,896,256]{2,1,0:T(8,128)(2,1)}, bf16[4,896,256]{2,1,0:T(8,128)(2,1)}, bf16[4,896,256]{2,1,0:T(8,...) custom-call(bf16[2,1568,256]{2,1,0:T(8,128)(2,1)} %bitcast.23, ...), custom_call_target="tpu_custom_call" | custom-call | tf_op jit(solution)/shard_map/block_forward/pallas_call | solution.py:237
  38.0 50.9 %decoder.1 = (bf16[512,512]{1,0:T(8,128)(2,1)}, f32[512,512]{1,0:T(8,128)}, bf16[4,896,512]{2,1,0:T(8,128)(2,1)}, bf16[12,512,512]{2,1,0:T(8,128)(2,1)}, f32[3,5...) custom-call(f32[3,512]{1,0:T(4,128)} %ln_gain.1, f32[3,512]{1,0:T(4,128)} %ln_bias.1, ...), custom_call_target="tpu_custom_call" | custom-call | tf_op jit(solution)/shard_map/decoder/pallas_call | solution.py:896
  88.9 109.6 %block_backward.1 = (bf16[8704,512]{1,0:T(8,128)(2,1)}, f32[16,512]{1,0:T(8,128)}, bf16[2,8,224,256]{3,2,1,0:T(8,128)(2,1)}) custom-call(bf16[4,896,512]{2,1,0:T(8,128)(2,1)} %get-tuple-element.63.grad_tokens, bf16[4,896,256]{2,1,0:T(8,128)(2,1)} %get-tuple-element.64.padded, bf16[4,896,256]{2,1,0:T(8,128)(2,1)} %get-tuple-element.65.hidden, ...), custom_call_target="tpu_custom_call" | custom-call | tf_op jit(solution)/shard_map/block_backward/pallas_call | solution.py:618
  198.5 12.7 %widen.1 = (f32[2,3,3,256,256]{4,3,2,1,0:T(8,128)}, f32[256,512]{1,0:T(8,128)}, f32[6,512,512]{2,1,0:T(8,128)}, f32[2,512,512]{2,1,0:T(8,128)}, f32[512,1024]{1,...) custom-call(f32[16,512]{1,0:T(8,128)} %get-tuple-element.76.small, ...), custom_call_target="tpu_custom_call" | custom-call | tf_op jit(solution)/shard_map/widen/pallas_call | solution.py:1038
